TPU v7x, 512 devices: a whole 4x4x16 slice. The times are simulated.
512 devices in a mesh: outer: 32 (over x_hi, z), inner: 16 (over y, x_lo, core).
Axes of the slice: x: 4 (x_hi: 2, x_lo: 2; x = x_hi * 2 + x_lo), y: 4, z: 16, core: 2. Of those that a mesh axis runs over, the one named last changes fastest.
Arguments:
- queries: bfloat16 [131072, 1024], P(('outer', 'inner')), may hold values from -10 to 10
- keys: bfloat16 [131072, 256], P(('outer', 'inner')), may hold values from -10 to 10
- values: bfloat16 [131072, 256], P(('outer', 'inner')), may hold values from -18 to 18
- pool_fine: float32 [16, 8], replicated, may hold values from -1.5 to 1.5
- pool_coarse: float32 [8, 8], replicated, may hold values from -2 to 2
- gain: float32 [1024], replicated, may hold values from 0.5 to 1.5
Outputs:
- normed: bfloat16 [131072, 1024], P(('outer', 'inner'))
All inputs are finite; a program needn't handle non-finite values.
Results may differ from a plain program's by a relative error of at most 0.008.
Values may be sent and summed in bfloat16 or wider, within the bound.
No kernel may reach another device: no remote copies, remote signals or barrier semaphores. Data moves between devices by JAX's collectives and lax.ppermute only.
A program may use at most 64 MiB of HBM per device.

v0:
```python
import jax
import jax.numpy as jnp
from jax import lax
from jax.sharding import Mesh
from jax.sharding import PartitionSpec as P

HQ = 16
KVH = 4
HD = 64
BLOCK = 512
FINE = 16
RATIO = 8
COARSE = 128
OUTER = ("outer_0", "outer_1")
OUTER_INNER = ("outer_0", "outer_1", "inner")


EPSILON = 1e-06
MASKED_SCORE = -1e30


def shifted(value, axis, steps):
    count = lax.axis_size(axis)
    first, last = (max(0, -steps), min(count, count - steps))
    return lax.ppermute(value, axis, [(source, source + steps) for source in range(first, last)])


def copy_for_each(array, axis):
    copies = jnp.broadcast_to(array, (lax.axis_size(axis), *array.shape))
    return lax.all_to_all(copies, axis, split_axis=0, concat_axis=0, tiled=True)


def joined_along(tiles, dim):
    tiles = jnp.moveaxis(tiles, 0, dim)
    lengths = tiles.shape
    return tiles.reshape(*lengths[:dim], lengths[dim] * lengths[dim + 1], *lengths[dim + 2 :])


def collect(array, axis, dim):
    tiles = copy_for_each(array, axis)
    return joined_along(tiles, dim)


def stacked_from(array, axes, turns):
    tiles = array
    for k in turns:
        tiles = lax.all_gather(tiles, axes[k])
    done = turns[::-1]
    back = [done.index(k) for k in range(len(axes))]
    tiles = tiles.transpose(*back, *range(len(axes), tiles.ndim))
    return tiles.reshape(-1, *array.shape)


def gather_axes(array, axes, turns, dim):
    return joined_along(stacked_from(array, axes, turns), dim)


def summarize(source, pooling, factor):
    amount = source.shape[0] // factor
    shaped = source.astype(jnp.float32).reshape(amount, factor, 2, KVH, HD)
    weights = pooling.reshape(factor, 2, KVH)
    pooled = jnp.einsum("mjskd,jsk->mskd", shaped, weights, precision=lax.Precision.HIGHEST)
    return pooled.reshape(amount, 2 * KVH * HD).astype(jnp.bfloat16)


def partial_state(stacked, keyset, allowed):
    amount = keyset.shape[0]
    kv_width = KVH * HD
    group_size = HQ // KVH
    tok_rows = allowed.shape[0]
    key_heads = keyset[:, :kv_width].reshape(amount, KVH, HD).transpose(1, 0, 2)
    value_heads = keyset[:, kv_width:].reshape(amount, KVH, HD).transpose(1, 0, 2)

    def one_group(group_idx):
        query_rows = lax.dynamic_index_in_dim(stacked, group_idx, 0, False)
        key_head = lax.dynamic_index_in_dim(key_heads, group_idx, 0, False)
        value_head = lax.dynamic_index_in_dim(value_heads, group_idx, 0, False)
        scores = lax.dot_general(
            query_rows, key_head, (((1,), (1,)), ((), ())), preferred_element_type=jnp.float32
        )
        scores = scores.reshape(group_size, tok_rows, amount)
        scores = jnp.where(allowed[None], scores * HD ** (-0.5), MASKED_SCORE)
        peak = jnp.max(scores, axis=2)
        expon = jnp.where(allowed[None], jnp.exp(scores - peak[..., None]), 0.0)
        totals = jnp.sum(expon, axis=2)
        weights = expon.astype(jnp.bfloat16).reshape(group_size * tok_rows, amount)
        blended = jnp.dot(weights, value_head, preferred_element_type=jnp.float32)
        return (peak.reshape(group_size * tok_rows), totals.reshape(group_size * tok_rows), blended)

    return lax.map(one_group, jnp.arange(KVH))


def merge_states(former, latter):
    peak = jnp.maximum(former[0], latter[0])
    leading = jnp.exp(former[0] - peak)
    trailing = jnp.exp(latter[0] - peak)
    totals = former[1] * leading + latter[1] * trailing
    blended = former[2] * leading[..., None] + latter[2] * trailing[..., None]
    return (peak, totals, blended)


def local(queries, keys, values, pool_fine, pool_coarse, gain):
    tok_dev = queries.shape[0]
    group_size = HQ // KVH
    inner_count = lax.axis_size("inner")
    devices_all = lax.axis_size(OUTER) * inner_count
    device = lax.axis_index(OUTER_INNER)
    group_index = lax.axis_index(OUTER)
    dev_start = device * tok_dev
    group_tok = tok_dev * inner_count
    query_block = (dev_start + jnp.arange(tok_dev)) // BLOCK
    stacked = (
        queries.reshape(tok_dev, KVH, group_size, HD)
        .transpose(1, 2, 0, 3)
        .reshape(KVH, group_size * tok_dev, HD)
    )
    paired = jnp.concatenate([keys, values], axis=1)
    reach = max(1, 2 * BLOCK // tok_dev - 1)
    offsets = list(range(reach, 0, -1)) + list(range(-1, -reach - 1, -1))
    shifted_parts = []
    for offset in offsets:
        shifted_parts.append(shifted(paired, OUTER_INNER, offset))
    window = jnp.concatenate(shifted_parts[:reach] + [paired] + shifted_parts[reach:], axis=0)
    key_pos = dev_start - reach * tok_dev + jnp.arange(window.shape[0])
    inside = (key_pos >= 0) & (key_pos < devices_all * tok_dev)
    near_ok = inside[None, :] & (jnp.abs(key_pos[None, :] // BLOCK - query_block[:, None]) <= 1)
    merged = partial_state(stacked, window, near_ok)
    fine_local = summarize(paired, pool_fine, FINE)
    group_fine = collect(fine_local, "inner", 0)
    fine_pos = group_index * group_tok + jnp.arange(group_fine.shape[0]) * FINE
    fine_ok = jnp.abs(fine_pos[None, :] // BLOCK - query_block[:, None]) > 1
    merged = merge_states(merged, partial_state(stacked, group_fine, fine_ok))
    coarse_group = summarize(group_fine, pool_coarse, RATIO)
    portion = gather_axes(coarse_group, OUTER, (0, 1), 0)
    coarse_pos = jnp.arange(portion.shape[0]) * COARSE
    far_group = (coarse_pos // group_tok != group_index)[None, :]
    merged = merge_states(
        merged,
        partial_state(
            stacked,
            portion,
            far_group & (jnp.abs(coarse_pos[None, :] // BLOCK - query_block[:, None]) > 1),
        ),
    )
    attended = merged[2] / merged[1][..., None]
    attended = (
        attended.reshape(KVH, group_size, tok_dev, HD)
        .transpose(2, 0, 1, 3)
        .reshape(tok_dev, HQ * HD)
    )
    rescale = lax.rsqrt(jnp.mean(attended * attended, axis=1, keepdims=True) + EPSILON)
    return (attended * rescale * gain).astype(jnp.bfloat16)


def solution(mesh):
    torus = Mesh(mesh.devices.reshape(2, 16, mesh.shape["inner"]), ("outer_0", "outer_1", "inner"))
    return jax.shard_map(
        local,
        mesh=torus,
        in_specs=(P(OUTER_INNER, None), P(OUTER_INNER, None), P(OUTER_INNER, None), P(), P(), P()),
        out_specs=P(OUTER_INNER, None),
        check_vma=False,
    )
```

profile of v0, /device:TPU:12, one launch (start us, length us, event | category | flops | bytes accessed | tf_op | source)
XLA Modules:
  0.0 185.5 jit_solution(764437504368639732)
XLA Ops:
  6.5 1.1 copy.51
  7.6 1.0 copy.52
  8.6 2.5 %collective-permute-start = (bf16[256,512]{0,1:T(8,128)(2,1)S(1)}, bf16[256,512]{0,1:T(8,128)(2,1)}, u32[]{:S(2)}, u32[]{:S(2)}) collective-permute-start(bf16[256,512]{0,1:T(8,128)(2,1)S(1)} %pad_maximum_fusion), channel_id=1, source_target_pairs={{0,3},{1,4},{2,5},{3,6},{4,7},{5,8},{6,9},{7,10},{8,11},{9,12},{10... | collective-permute-start | bytes 786440 | tf_op jit(solution)/shard_map/ppermute | solution.py:25
  11.2 3.8 %collective-permute-start.1 = (bf16[256,512]{0,1:T(8,128)(2,1)S(1)}, bf16[256,512]{0,1:T(8,128)(2,1)}, u32[]{:S(2)}, u32[]{:S(2)}) collective-permute-start(bf16[256,512]{0,1:T(8,128)(2,1)S(1)} %pad_maximum_fusion), channel_id=1, source_target_pairs={{0,2},{1,3},{2,4},{3,5},{4,6},{5,7},{6,8},{7,9},{8,10},{9,11},{10,... | collective-permute-start | bytes 786440 | tf_op jit(solution)/shard_map/ppermute | solution.py:25
  15.0 2.1 %collective-permute-start.2 = (bf16[256,512]{0,1:T(8,128)(2,1)S(1)}, bf16[256,512]{0,1:T(8,128)(2,1)}, u32[]{:S(2)}, u32[]{:S(2)}) collective-permute-start(bf16[256,512]{0,1:T(8,128)(2,1)S(1)} %pad_maximum_fusion), channel_id=1, source_target_pairs={{0,1},{1,2},{2,3},{3,4},{4,5},{5,6},{6,7},{7,8},{8,9},{9,10},{10,1... | collective-permute-start | bytes 786440 | tf_op jit(solution)/shard_map/ppermute | solution.py:25
  17.0 4.4 %collective-permute-start.3 = (bf16[256,512]{0,1:T(8,128)(2,1)S(1)}, bf16[256,512]{0,1:T(8,128)(2,1)}, u32[]{:S(2)}, u32[]{:S(2)}) collective-permute-start(bf16[256,512]{0,1:T(8,128)(2,1)S(1)} %pad_maximum_fusion), channel_id=1, source_target_pairs={{1,0},{2,1},{3,2},{4,3},{5,4},{6,5},{7,6},{8,7},{9,8},{10,9},{11,1... | collective-permute-start | bytes 786440 | tf_op jit(solution)/shard_map/ppermute | solution.py:25
  21.4 2.1 %collective-permute-start.4 = (bf16[256,512]{0,1:T(8,128)(2,1)S(1)}, bf16[256,512]{0,1:T(8,128)(2,1)S(1)}, u32[]{:S(2)}, u32[]{:S(2)}) collective-permute-start(bf16[256,512]{0,1:T(8,128)(2,1)S(1)} %pad_maximum_fusion), channel_id=1, source_target_pairs={{2,0},{3,1},{4,2},{5,3},{6,4},{7,5},{8,6},{9,7},{10,8},{11,9},{12,... | collective-permute-start | bytes 786440 | tf_op jit(solution)/shard_map/ppermute | solution.py:25
  25.2 12.2 %all-to-all-start = ((bf16[16,16,512]{2,1,0:T(8,128)(2,1)}), bf16[16,16,512]{2,1,0:T(8,128)(2,1)S(1)}, u32[]{:S(2)}, u32[]{:S(2)}) async-start(bf16[16,16,512]{2,1,0:T(8,128)(2,1)} %broadcast_in_dim.110), calls=%async_computation | async-start | bytes 524288 | tf_op jit(solution)/shard_map/all_to_all | solution.py:30
  37.9 5.0 %all-to-all-done = bf16[16,16,512]{2,1,0:T(8,128)(2,1)S(1)} async-done(((bf16[16,16,512]{2,1,0:T(8,128)(2,1)}), bf16[16,16,512]{2,1,0:T(8,128)(2,1)S(1)}, u32[]{:S(2)}, u32[]{:S(2)}) %all-to-all-start) | async-done | bytes 262176 | tf_op jit(solution)/shard_map/all_to_all | solution.py:30
  43.3 16.6 %while.46 = (s32[]{:T(128)}, f32[4,1024]{1,0:T(4,128)S(1)}, f32[4,1024]{1,0:T(4,128)S(1)}, f32[4,1024,64]{1,2,0:T(8,128)S(1)}, s32[4]{0:T(128)S(1)}, /*index=5*/...) while((s32[]{:T(128)}, f32[4,1024]{1,0:T(4,128)S(1)}, ...), condition=%wide.region_7.8_spmd.clone, body=%wide.region_4.7_spmd.clone.sunk | while | flops 69138432 | bytes 4372675 | solution.py:90
  61.0 6.3 %all_gather.10 = bf16[2,32,512]{2,1,0:T(8,128)(2,1)} all-gather(bf16[1,32,512]{2,1,0:T(8,128)(2,1)S(1)} %convert_element_type.44), channel_id=1, replica_groups=mesh['outer_0'=2,'outer_1'=16,'inner'=16] {'outer_0'}, dimensions={0}, use_global_device_ids=true | all-gather | bytes 98304 | tf_op jit(solution)/shard_map/all_gather | solution.py:47
  67.4 2.6 %collective-permute-start.5 = (bf16[256,512]{0,1:T(8,128)(2,1)S(1)}, bf16[256,512]{0,1:T(8,128)(2,1)S(1)}, u32[]{:S(2)}, u32[]{:S(2)}) collective-permute-start(bf16[256,512]{0,1:T(8,128)(2,1)S(1)} %pad_maximum_fusion), channel_id=1, source_target_pairs={{3,0},{4,1},{5,2},{6,3},{7,4},{8,5},{9,6},{10,7},{11,8},{12,9},{13... | collective-permute-start | bytes 786440 | tf_op jit(solution)/shard_map/ppermute | solution.py:25
  70.0 1.0 constant_dynamic-update-slice_fusion.6
  71.0 1.0 constant_dynamic-update-slice_fusion.5
  71.9 1.0 constant_dynamic-update-slice_fusion.4
  72.9 1.0 constant_dynamic-update-slice_fusion.2
  74.0 1.1 collective-permute-done.5
  75.1 1.1 fusion.68
  76.2 1.1 broadcast.256.clone.2
  77.3 40.6 %while.45 = (s32[]{:T(128)}, f32[4,1024]{1,0:T(4,128)S(1)}, f32[4,1024]{1,0:T(4,128)S(1)}, f32[4,1024,64]{1,2,0:T(8,128)}, s32[4]{0:T(128)S(1)}, /*index=5*/bf16...) while((s32[]{:T(128)}, f32[4,1024]{1,0:T(4,128)S(1)}, ...), condition=%wide.region_3.4_spmd.clone, body=%wide.region_0.3_spmd.clone.sunk | while | flops 488110080 | bytes 24828360 | solution.py:90
  80.5 2.5 %fusion.96 = (f32[4,256]{1,0:T(4,128)S(1)}, f32[4,256,1792]{2,1,0:T(8,128)S(1)}) fusion(pred[256,1792]{1,0:T(8,128)(4,1)S(1)} %fusion.95, bf16[4,1792,64]{1,2,0:T(8,128)(2,1)} %get-tuple-element.758, s32[]{:T(128)S(6)} %select_n.155, bf16[4,256,64]{1,0,2:T(4,128)(2,1)S(1)} %dot_general.44), kind=kOutput, calls=%fused_computation.5.clone.1 | convolution fusion | flops 240385024 | bytes 8163332 | tf_op jit(solution)/shard_map/while/body/eval_jaxpr/dot_general | solution.py:78
  83.0 2.3 %fusion.97 = (bf16[4,256,1792]{2,1,0:T(8,128)(2,1)S(1)}, f32[4,256]{1,0:T(4,128)S(1)}) fusion(f32[4,256,1792]{2,1,0:T(8,128)S(1)} %get-tuple-element.611, f32[4,256]{1,0:T(4,128)S(1)} %get-tuple-element.610, pred[256,1792]{1,0:T(8,128)(4,1)S(1)} %fusion.95), kind=kLoop, calls=%fused_computation.6.clone.1 | loop fusion | flops 11009024 | bytes 11476992 | tf_op jit(solution)/shard_map/while/body/eval_jaxpr/convert_element_type | solution.py:86
  85.4 1.9 %fusion.98 = f32[4,1024,64]{1,2,0:T(8,128)} fusion(f32[4,1024,64]{1,2,0:T(8,128)} %get-tuple-element.741, s32[]{:T(128)} %get-tuple-element.738, bf16[1024,1792]{1,0:T(8,128)(2,1)S(1)} %bitcast.202, bf16[4,1792,64]{1,2,0:T(8,128)(2,1)S(1)} %get-tuple-element.759, s32[]{:T(128)S(6)} %select_n.155), kind=kOutput, calls=%fused_computation.11.clone.1 | convolution fusion | flops 234881024 | bytes 4162052 | tf_op jit(solution)/shard_map/while/body/eval_jaxpr/dot_general | solution.py:87
  90.7 2.5 %fusion.96 = (f32[4,256]{1,0:T(4,128)S(1)}, f32[4,256,1792]{2,1,0:T(8,128)S(1)}) fusion(pred[256,1792]{1,0:T(8,128)(4,1)S(1)} %fusion.95, bf16[4,1792,64]{1,2,0:T(8,128)(2,1)} %get-tuple-element.758, s32[]{:T(128)S(6)} %select_n.155, bf16[4,256,64]{1,0,2:T(4,128)(2,1)S(1)} %dot_general.44), kind=kOutput, calls=%fused_computation.5.clone.1 | convolution fusion | flops 240385024 | bytes 8163332 | tf_op jit(solution)/shard_map/while/body/eval_jaxpr/dot_general | solution.py:78
  93.2 2.3 %fusion.97 = (bf16[4,256,1792]{2,1,0:T(8,128)(2,1)S(1)}, f32[4,256]{1,0:T(4,128)S(1)}) fusion(f32[4,256,1792]{2,1,0:T(8,128)S(1)} %get-tuple-element.611, f32[4,256]{1,0:T(4,128)S(1)} %get-tuple-element.610, pred[256,1792]{1,0:T(8,128)(4,1)S(1)} %fusion.95), kind=kLoop, calls=%fused_computation.6.clone.1 | loop fusion | flops 11009024 | bytes 11476992 | tf_op jit(solution)/shard_map/while/body/eval_jaxpr/convert_element_type | solution.py:86
  95.5 1.9 %fusion.98 = f32[4,1024,64]{1,2,0:T(8,128)} fusion(f32[4,1024,64]{1,2,0:T(8,128)} %get-tuple-element.741, s32[]{:T(128)} %get-tuple-element.738, bf16[1024,1792]{1,0:T(8,128)(2,1)S(1)} %bitcast.202, bf16[4,1792,64]{1,2,0:T(8,128)(2,1)S(1)} %get-tuple-element.759, s32[]{:T(128)S(6)} %select_n.155), kind=kOutput, calls=%fused_computation.11.clone.1 | convolution fusion | flops 234881024 | bytes 4162052 | tf_op jit(solution)/shard_map/while/body/eval_jaxpr/dot_general | solution.py:87
  100.9 2.5 %fusion.96 = (f32[4,256]{1,0:T(4,128)S(1)}, f32[4,256,1792]{2,1,0:T(8,128)S(1)}) fusion(pred[256,1792]{1,0:T(8,128)(4,1)S(1)} %fusion.95, bf16[4,1792,64]{1,2,0:T(8,128)(2,1)} %get-tuple-element.758, s32[]{:T(128)S(6)} %select_n.155, bf16[4,256,64]{1,0,2:T(4,128)(2,1)S(1)} %dot_general.44), kind=kOutput, calls=%fused_computation.5.clone.1 | convolution fusion | flops 240385024 | bytes 8163332 | tf_op jit(solution)/shard_map/while/body/eval_jaxpr/dot_general | solution.py:78
  103.4 2.3 %fusion.97 = (bf16[4,256,1792]{2,1,0:T(8,128)(2,1)S(1)}, f32[4,256]{1,0:T(4,128)S(1)}) fusion(f32[4,256,1792]{2,1,0:T(8,128)S(1)} %get-tuple-element.611, f32[4,256]{1,0:T(4,128)S(1)} %get-tuple-element.610, pred[256,1792]{1,0:T(8,128)(4,1)S(1)} %fusion.95), kind=kLoop, calls=%fused_computation.6.clone.1 | loop fusion | flops 11009024 | bytes 11476992 | tf_op jit(solution)/shard_map/while/body/eval_jaxpr/convert_element_type | solution.py:86
  105.7 1.9 %fusion.98 = f32[4,1024,64]{1,2,0:T(8,128)} fusion(f32[4,1024,64]{1,2,0:T(8,128)} %get-tuple-element.741, s32[]{:T(128)} %get-tuple-element.738, bf16[1024,1792]{1,0:T(8,128)(2,1)S(1)} %bitcast.202, bf16[4,1792,64]{1,2,0:T(8,128)(2,1)S(1)} %get-tuple-element.759, s32[]{:T(128)S(6)} %select_n.155), kind=kOutput, calls=%fused_computation.11.clone.1 | convolution fusion | flops 234881024 | bytes 4162052 | tf_op jit(solution)/shard_map/while/body/eval_jaxpr/dot_general | solution.py:87
  111.0 2.5 %fusion.96 = (f32[4,256]{1,0:T(4,128)S(1)}, f32[4,256,1792]{2,1,0:T(8,128)S(1)}) fusion(pred[256,1792]{1,0:T(8,128)(4,1)S(1)} %fusion.95, bf16[4,1792,64]{1,2,0:T(8,128)(2,1)} %get-tuple-element.758, s32[]{:T(128)S(6)} %select_n.155, bf16[4,256,64]{1,0,2:T(4,128)(2,1)S(1)} %dot_general.44), kind=kOutput, calls=%fused_computation.5.clone.1 | convolution fusion | flops 240385024 | bytes 8163332 | tf_op jit(solution)/shard_map/while/body/eval_jaxpr/dot_general | solution.py:78
  113.5 2.3 %fusion.97 = (bf16[4,256,1792]{2,1,0:T(8,128)(2,1)S(1)}, f32[4,256]{1,0:T(4,128)S(1)}) fusion(f32[4,256,1792]{2,1,0:T(8,128)S(1)} %get-tuple-element.611, f32[4,256]{1,0:T(4,128)S(1)} %get-tuple-element.610, pred[256,1792]{1,0:T(8,128)(4,1)S(1)} %fusion.95), kind=kLoop, calls=%fused_computation.6.clone.1 | loop fusion | flops 11009024 | bytes 11476992 | tf_op jit(solution)/shard_map/while/body/eval_jaxpr/convert_element_type | solution.py:86
  115.8 1.9 %fusion.98 = f32[4,1024,64]{1,2,0:T(8,128)} fusion(f32[4,1024,64]{1,2,0:T(8,128)} %get-tuple-element.741, s32[]{:T(128)} %get-tuple-element.738, bf16[1024,1792]{1,0:T(8,128)(2,1)S(1)} %bitcast.202, bf16[4,1792,64]{1,2,0:T(8,128)(2,1)S(1)} %get-tuple-element.759, s32[]{:T(128)S(6)} %select_n.155), kind=kOutput, calls=%fused_computation.11.clone.1 | convolution fusion | flops 234881024 | bytes 4162052 | tf_op jit(solution)/shard_map/while/body/eval_jaxpr/dot_general | solution.py:87
  117.9 22.2 %all-gather.3.cloned.1.call-done = bf16[32,32,512]{2,1,0:T(8,128)(2,1)} async-done(((bf16[2,32,512]{2,1,0:T(8,128)(2,1)}), bf16[32,32,512]{2,1,0:T(8,128)(2,1)}) %all-gather.3.cloned.1.call-update) | async-done | bytes 1048592 | tf_op jit(solution)/shard_map/all_gather | solution.py:47
  140.1 1.3 copy.59
  141.5 1.0 copy.60
  142.9 29.7 %while.47 = (s32[]{:T(128)}, f32[4,1024]{1,0:T(4,128)S(1)}, f32[4,1024]{1,0:T(4,128)S(1)}, f32[4,1024,64]{1,2,0:T(8,128)S(1)}, s32[4]{0:T(128)S(1)}, /*index=5*/...) while((s32[]{:T(128)}, f32[4,1024]{1,0:T(4,128)S(1)}, ...), condition=%wide.region_11.12_spmd.clone, body=%wide.region_8.11_spmd.clone.sunk | while | flops 278919168 | bytes 14600395 | solution.py:90
  145.9 1.9 %fusion.107 = (f32[4,256]{1,0:T(4,128)S(1)}, f32[4,256,1024]{2,1,0:T(8,128)S(1)}) fusion(pred[256,1024]{1,0:T(8,128)(4,1)S(1)} %fusion.106, bf16[4,1024,64]{1,2,0:T(8,128)(2,1)} %get-tuple-element.677, s32[]{:T(128)S(6)} %select_n.161, bf16[4,256,64]{1,0,2:T(4,128)(2,1)S(1)} %dot_general.46), kind=kOutput, calls=%fused_computation.39.clone.1 | convolution fusion | flops 137362432 | bytes 4722692 | tf_op jit(solution)/shard_map/while/body/eval_jaxpr/dot_general | solution.py:78
  147.8 1.5 fusion.108
  149.4 0.8 fusion.109
  153.4 1.9 %fusion.107 = (f32[4,256]{1,0:T(4,128)S(1)}, f32[4,256,1024]{2,1,0:T(8,128)S(1)}) fusion(pred[256,1024]{1,0:T(8,128)(4,1)S(1)} %fusion.106, bf16[4,1024,64]{1,2,0:T(8,128)(2,1)} %get-tuple-element.677, s32[]{:T(128)S(6)} %select_n.161, bf16[4,256,64]{1,0,2:T(4,128)(2,1)S(1)} %dot_general.46), kind=kOutput, calls=%fused_computation.39.clone.1 | convolution fusion | flops 137362432 | bytes 4722692 | tf_op jit(solution)/shard_map/while/body/eval_jaxpr/dot_general | solution.py:78
  155.2 1.5 fusion.108
  160.8 1.9 %fusion.107 = (f32[4,256]{1,0:T(4,128)S(1)}, f32[4,256,1024]{2,1,0:T(8,128)S(1)}) fusion(pred[256,1024]{1,0:T(8,128)(4,1)S(1)} %fusion.106, bf16[4,1024,64]{1,2,0:T(8,128)(2,1)} %get-tuple-element.677, s32[]{:T(128)S(6)} %select_n.161, bf16[4,256,64]{1,0,2:T(4,128)(2,1)S(1)} %dot_general.46), kind=kOutput, calls=%fused_computation.39.clone.1 | convolution fusion | flops 137362432 | bytes 4722692 | tf_op jit(solution)/shard_map/while/body/eval_jaxpr/dot_general | solution.py:78
  162.6 1.5 fusion.108
  168.2 1.9 %fusion.107 = (f32[4,256]{1,0:T(4,128)S(1)}, f32[4,256,1024]{2,1,0:T(8,128)S(1)}) fusion(pred[256,1024]{1,0:T(8,128)(4,1)S(1)} %fusion.106, bf16[4,1024,64]{1,2,0:T(8,128)(2,1)} %get-tuple-element.677, s32[]{:T(128)S(6)} %select_n.161, bf16[4,256,64]{1,0,2:T(4,128)(2,1)S(1)} %dot_general.46), kind=kOutput, calls=%fused_computation.39.clone.1 | convolution fusion | flops 137362432 | bytes 4722692 | tf_op jit(solution)/shard_map/while/body/eval_jaxpr/dot_general | solution.py:78
  170.1 1.5 fusion.108
  172.6 2.6 %add_divide_fusion = f32[4,1024,64]{1,2,0:T(8,128)} fusion(f32[4,1024,64]{1,2,0:T(8,128)S(1)} %get-tuple-element.157, f32[4,1024,64]{1,2,0:T(8,128)S(1)} %get-tuple-element.155, f32[4,1024,64]{1,2,0:T(8,128)} %get-tuple-element.152, f32[4,1024]{1,0:T(4,128)S(1)} %get-tuple-element.399, f32[4,1024]{1,0:T(4,128)S(1)} %get-tuple-element.403, ...), kind=kLoop, calls=%fused_computation.59 | loop fusion | flops 1835008 | bytes 4276224 | tf_op jit(solution)/shard_map/div | solution.py:145
  175.2 1.7 reshape.272
  177.6 1.0 copy.64
  (169 shorter events, 26.3 us)
Async XLA Ops:
  6.5 17.4 %copy-start = (f32[16,8]{0,1:T(8,128)S(1)}, f32[16,8]{0,1:T(8,128)}, u32[]{:S(2)}) copy-start(f32[16,8]{0,1:T(8,128)} %param.15) | copy-start | bytes 1540
  6.5 31.0 %copy-start.1 = (bf16[256,1024]{1,0:T(8,128)(2,1)S(1)}, bf16[256,1024]{1,0:T(8,128)(2,1)}, u32[]{:S(2)}) copy-start(bf16[256,1024]{1,0:T(8,128)(2,1)} %param.12) | copy-start | bytes 1572868
  6.5 31.2 %copy-start.3 = (f32[8,8]{1,0:T(8,128)S(1)}, f32[8,8]{1,0:T(8,128)}, u32[]{:S(2)}) copy-start(f32[8,8]{1,0:T(8,128)} %param.16) | copy-start | bytes 772
  8.6 58.7 %collective-permute-start = (bf16[256,512]{0,1:T(8,128)(2,1)S(1)}, bf16[256,512]{0,1:T(8,128)(2,1)}, u32[]{:S(2)}, u32[]{:S(2)}) collective-permute-start(bf16[256,512]{0,1:T(8,128)(2,1)S(1)} %pad_maximum_fusion), channel_id=1, source_target_pairs={{0,3},{1,4},{2,5},{3,6},{4,7},{5,8},{6,9},{7,10},{8,11},{9,12},{10... | collective-permute-start | bytes 786440 | tf_op jit(solution)/shard_map/ppermute | solution.py:25
  11.2 59.7 %collective-permute-start.1 = (bf16[256,512]{0,1:T(8,128)(2,1)S(1)}, bf16[256,512]{0,1:T(8,128)(2,1)}, u32[]{:S(2)}, u32[]{:S(2)}) collective-permute-start(bf16[256,512]{0,1:T(8,128)(2,1)S(1)} %pad_maximum_fusion), channel_id=1, source_target_pairs={{0,2},{1,3},{2,4},{3,5},{4,6},{5,7},{6,8},{7,9},{8,10},{9,11},{10,... | collective-permute-start | bytes 786440 | tf_op jit(solution)/shard_map/ppermute | solution.py:25
  15.0 57.0 %collective-permute-start.2 = (bf16[256,512]{0,1:T(8,128)(2,1)S(1)}, bf16[256,512]{0,1:T(8,128)(2,1)}, u32[]{:S(2)}, u32[]{:S(2)}) collective-permute-start(bf16[256,512]{0,1:T(8,128)(2,1)S(1)} %pad_maximum_fusion), channel_id=1, source_target_pairs={{0,1},{1,2},{2,3},{3,4},{4,5},{5,6},{6,7},{7,8},{8,9},{9,10},{10,1... | collective-permute-start | bytes 786440 | tf_op jit(solution)/shard_map/ppermute | solution.py:25
  17.0 55.9 %collective-permute-start.3 = (bf16[256,512]{0,1:T(8,128)(2,1)S(1)}, bf16[256,512]{0,1:T(8,128)(2,1)}, u32[]{:S(2)}, u32[]{:S(2)}) collective-permute-start(bf16[256,512]{0,1:T(8,128)(2,1)S(1)} %pad_maximum_fusion), channel_id=1, source_target_pairs={{1,0},{2,1},{3,2},{4,3},{5,4},{6,5},{7,6},{8,7},{9,8},{10,9},{11,1... | collective-permute-start | bytes 786440 | tf_op jit(solution)/shard_map/ppermute | solution.py:25
  21.4 52.5 %collective-permute-start.4 = (bf16[256,512]{0,1:T(8,128)(2,1)S(1)}, bf16[256,512]{0,1:T(8,128)(2,1)S(1)}, u32[]{:S(2)}, u32[]{:S(2)}) collective-permute-start(bf16[256,512]{0,1:T(8,128)(2,1)S(1)} %pad_maximum_fusion), channel_id=1, source_target_pairs={{2,0},{3,1},{4,2},{5,3},{6,4},{7,5},{8,6},{9,7},{10,8},{11,9},{12,... | collective-permute-start | bytes 786440 | tf_op jit(solution)/shard_map/ppermute | solution.py:25
  25.2 17.7 %all-to-all-start = ((bf16[16,16,512]{2,1,0:T(8,128)(2,1)}), bf16[16,16,512]{2,1,0:T(8,128)(2,1)S(1)}, u32[]{:S(2)}, u32[]{:S(2)}) async-start(bf16[16,16,512]{2,1,0:T(8,128)(2,1)} %broadcast_in_dim.110), calls=%async_computation | async-start | bytes 524288 | tf_op jit(solution)/shard_map/all_to_all | solution.py:30
  37.4 102.8 %all-gather.3.cloned.1.call-start = ((), (), s32[]{:S(2)}) async-start(), calls=%async_computation.1 | async-start | bytes 1114112 | tf_op jit(solution)/shard_map/all_gather | solution.py:47
  67.4 7.7 %collective-permute-start.5 = (bf16[256,512]{0,1:T(8,128)(2,1)S(1)}, bf16[256,512]{0,1:T(8,128)(2,1)S(1)}, u32[]{:S(2)}, u32[]{:S(2)}) collective-permute-start(bf16[256,512]{0,1:T(8,128)(2,1)S(1)} %pad_maximum_fusion), channel_id=1, source_target_pairs={{3,0},{4,1},{5,2},{6,3},{7,4},{8,5},{9,6},{10,7},{11,8},{12,9},{13... | collective-permute-start | bytes 786440 | tf_op jit(solution)/shard_map/ppermute | solution.py:25
  175.2 2.2 %copy-start.2 = (f32[1024]{0:T(1024)S(1)}, f32[1024]{0:T(1024)}, u32[]{:S(2)}) copy-start(f32[1024]{0:T(1024)} %param.17) | copy-start | bytes 12292
Sparse Core Ops, SparseCore 0:
  67.5 72.6 all-gather.2
where the time goes:
time: 187 us; the launch traced here: 185 us
  matrix products  31.9 us (17%)
  starting transfers between devices  29.7 us (16%)
  waiting for transfers between devices  28.4 us (15%)
  local copies, waits for them, and re-layouts  26.4 us (14%)
  other arithmetic  25 us (13%)
  loops' own time  24 us (13%)
  between operations  13.8 us (7%)
  blocking collectives  6.34 us (3%)
    another operation x3, loops' own time, partial_state(): return lax.map(one_group, jnp.arange(KVH))  24 us
    all_gather x1, waiting for transfers between devices, stacked_from(): tiles = lax.all_gather(tiles, axes[k])  22.2 us
    dot_general x12, matrix products, one_group(): lax.dot_general(query_rows, key_head, (((1,), (1,)), ((), ())), preferred...  19.1 us
    ppermute x6, starting transfers between devices, shifted(): lax.ppermute(value, axis, [(source, source + steps) for source in range(f...  17.4 us
    convert_element_type x12, other arithmetic, one_group(): weights = expon.astype(jnp.bfloat16).reshape(group_size * tok_rows, amount)  17.3 us
    all_to_all x1, starting transfers between devices, copy_for_each(): return lax.all_to_all(copies, axis, split_axis=0, concat_axis=0, tiled=True)  12.2 us
    dot_general x12, matrix products, one_group(): blended = jnp.dot(weights, value_head, preferred_element_type=jnp.float32)  11.9 us
    dynamic_slice x12, local copies, waits for them, and re-layouts, partial_state(): return lax.map(one_group, jnp.arange(KVH))  7.3 us
  transfers between devices with their start and end apart: 8, of which 3 were waited for; matrix products, arithmetic and copies ran while one was open for 27% of the time, Pallas kernels for 0%

commit v1 on v0

v1 whole, which is shorter than its diff:
```python
import jax
import jax.numpy as jnp
from jax import lax
from jax.experimental import pallas as pl
from jax.experimental.pallas import tpu as pltpu
from jax.sharding import Mesh
from jax.sharding import PartitionSpec as P

HQ = 16
KVH = 4
HD = 64
BLOCK = 512
FINE = 16
RATIO = 8
D = 1024
TOK = 256
HALF = 512
ZN = 16
GROUPS = 32
INNERS = 16
ZROWS = 8
ALL = ("o0", "z", "y", "xl", "c")
OUTER = ("o0", "z")
INNER = ("y", "xl", "c")
EPSILON = 1e-06
VMEM = pltpu.VMEM
SMEM = pltpu.SMEM
F32 = jnp.float32
BF16 = jnp.bfloat16


def params(mebibytes=48):
    return pltpu.CompilerParams(vmem_limit_bytes=int(mebibytes * 1024 * 1024))


def vmem_spec():
    return pl.BlockSpec(memory_space=VMEM)


def smem_spec():
    return pl.BlockSpec(memory_space=SMEM)


def hbm_spec():
    return pl.BlockSpec(memory_space=pltpu.HBM)


def widen(w, part_dim):
    part = lax.broadcasted_iota(jnp.int32, (2 * KVH, 2 * KVH * HD), 0)
    lane = lax.broadcasted_iota(jnp.int32, (2 * KVH, 2 * KVH * HD), 1)
    pick = jnp.where(lane // HD == part, 1.0, 0.0)
    return lax.dot_general(
        w, pick, (((part_dim,), (0,)), ((), ())), precision=lax.Precision.HIGHEST, preferred_element_type=F32
    )


def begin_kernel(
    core_ref, q_hbm, k_hbm, v_hbm, wf_hbm, wc_hbm, fine_ref, coarse_ref, send_ref, qm_ref, kvm_ref, k_s, v_s, wf_s, wc_s, sems
):
    pairs = [(wf_hbm, wf_s), (wc_hbm, wc_s), (k_hbm, k_s), (v_hbm, v_s)]
    mine = core_ref[0]
    for src, width, at in ((q_hbm, HALF, 256), (k_hbm, 128, 0), (v_hbm, 128, 128)):
        for which, dst in ((1 - mine, send_ref), (mine, kvm_ref if width == 128 else qm_ref)):
            cols = pl.ds(pl.multiple_of(which * width, 128), width)
            start = 0 if dst is qm_ref else at
            pairs.append((src.at[:, cols], dst.at[:, start : start + width]))
    copies = [pltpu.make_async_copy(src, dst, sems.at[i]) for i, (src, dst) in enumerate(pairs)]
    for copy in copies:
        copy.start()
    copies[0].wait()
    copies[1].wait()
    wf = widen(wf_s[...], 0)
    wc = widen(wc_s[...], 1)
    if ZROWS > 8:
        coarse_ref[:, 8:, :] = jnp.zeros((GROUPS, ZROWS - 8, 128), BF16)
    for kv in range(2):
        copies[2 + kv].wait()
        cols = slice(kv * 256, (kv + 1) * 256)
        x = (k_s, v_s)[kv][...].astype(F32).reshape(TOK // FINE, FINE, 256)
        fine = jnp.sum(x * wf[None, :, cols], axis=1).astype(BF16)
        f = fine.astype(F32).reshape(2, RATIO, 256)
        coarse = jnp.sum(f * wc[None, :, cols], axis=1)
        for i in range(2):
            part = 2 * kv + i
            fine_ref[part] = fine[:, i * 128 : (i + 1) * 128]
            rows = jnp.broadcast_to(coarse[None, :, i * 128 : (i + 1) * 128], (GROUPS, 2, 128))
            coarse_ref[:, 2 * part : 2 * part + 2, :] = rows.astype(BF16)
    for copy in copies[4:]:
        copy.wait()


def begin(core, queries, keys, values, pool_fine, pool_coarse):
    return pl.pallas_call(
        begin_kernel,
        out_shape=(
            jax.ShapeDtypeStruct((4, TOK // FINE, 128), BF16),
            jax.ShapeDtypeStruct((GROUPS, ZROWS, 128), BF16),
            jax.ShapeDtypeStruct((TOK, 768), BF16),
            jax.ShapeDtypeStruct((TOK, HALF), BF16),
            jax.ShapeDtypeStruct((TOK, 256), BF16),
        ),
        in_specs=[smem_spec()] + [hbm_spec()] * 5,
        out_specs=(vmem_spec(),) * 5,
        scratch_shapes=[
            VMEM((TOK, 256), BF16),
            VMEM((TOK, 256), BF16),
            VMEM((2 * KVH, FINE), F32),
            VMEM((RATIO, 2 * KVH), F32),
            pltpu.SemaphoreType.DMA((10,)),
        ],
        compiler_params=params(54),
    )(core, queries, keys, values, pool_fine.T, pool_coarse)


NFINE = 256
NCOARSE = 1024
NFAR = NFINE + NCOARSE
LIMIT = 40.0


def cost(keys, times=1):
    return pl.CostEstimate(
        flops=8 * BLOCK * keys * 128 * 4 * times, bytes_accessed=4 << 20, transcendentals=8 * BLOCK * keys
    )


def swapped(x):
    return jnp.concatenate([x[:, 64:], x[:, :64]], axis=1)


def is_low(rows):
    return lax.broadcasted_iota(jnp.int32, (rows, 128), 1) < 64


def scores_of(q, k):
    return lax.dot_general(q, k, (((1,), (1,)), ((), ())), preferred_element_type=F32)


def first_lane(rows, keep=None):
    one = lax.broadcasted_iota(jnp.int32, (rows, 128), 1) == 0
    if keep is not None:
        one = one & keep
    return jnp.where(one, 1.0, 0.0).astype(BF16)


def fine_keep(group, block):
    row = lax.broadcasted_iota(jnp.int32, (NFINE, 128), 0)
    src_block = group * 8 + row // 32
    return jnp.abs(src_block - block) > 1


def coarse_keep(group, block):
    row = lax.broadcasted_iota(jnp.int32, (NCOARSE, 128), 0)
    src_group = (row // 2) % GROUPS
    src_block = src_group * 8 + row // 128
    return (src_group != group) & (jnp.abs(src_block - block) > 1)


def prep_kernel(place_ref, qm_ref, got_ref, q_ref, keep_ref):
    group = place_ref[0]
    block = place_ref[1]
    keep_ref[0:NFINE, :] = jnp.where(fine_keep(group, block), 1.0, 0.0).astype(BF16)
    keep_ref[NFINE:, :] = jnp.where(coarse_keep(group, block), 1.0, 0.0).astype(BF16)
    low = is_low(TOK)
    for ref, first, at in ((qm_ref, 0, 0), (got_ref, 256, TOK)):
        pairs = [ref[:, first + j * 128 : first + (j + 1) * 128].astype(F32) * HD ** (-0.5) for j in range(4)]
        other = [swapped(x) for x in pairs]
        for j in range(2):
            rows = slice(at, at + TOK)
            q_ref[2 * j, rows, :] = jnp.where(low, pairs[j], other[j + 2]).astype(BF16)
            q_ref[2 * j + 1, rows, :] = jnp.where(low, other[j], pairs[j + 2]).astype(BF16)


def prep(place, qm, got):
    return pl.pallas_call(
        prep_kernel,
        out_shape=(
            jax.ShapeDtypeStruct((4, BLOCK, 128), BF16),
            jax.ShapeDtypeStruct((NFAR, 128), BF16),
        ),
        in_specs=[smem_spec()] + [vmem_spec()] * 2,
        out_specs=(vmem_spec(), vmem_spec()),
        compiler_params=params(),
        cost_estimate=cost(3 * BLOCK),
    )(place, qm, got)


def of_head(pair, g, low):
    zero = jnp.zeros_like(pair)
    return jnp.where(low, pair, zero) if g == 0 else jnp.where(low, zero, pair)


def near_kernel(place_ref, kv_ref, prev_ref, next_ref, q_ref, o_out, ml_out, o_s, ml_s, k_s, v_s, sems):
    k_s[0:BLOCK, :] = kv_ref[:, :128]
    v_s[0:BLOCK, :128] = kv_ref[:, 128:]
    v_s[0:BLOCK, 128:] = first_lane(BLOCK)
    for i, ref in enumerate((prev_ref, next_ref)):
        rows = slice(BLOCK * (i + 1), BLOCK * (i + 2))
        valid = place_ref[2 + i] > 0

        @pl.when(valid)
        def _(ref=ref, rows=rows):
            k_s[rows, :] = ref[:, :128]
            v_s[rows, :128] = ref[:, 128:]
            v_s[rows, 128:] = first_lane(BLOCK)

        @pl.when(jnp.logical_not(valid))
        def _(rows=rows):
            k_s[rows, :] = k_s[0:BLOCK, :]
            v_s[rows, :] = jnp.zeros((BLOCK, 256), BF16)

    low = is_low(TOK)
    lane = lax.broadcasted_iota(jnp.int32, (TOK, 128), 1)
    copies = []
    sides = [jnp.zeros((TOK, 128), F32)] * 2
    for i in range(4):
        for t in range(2):
            rows = slice(t * TOK, (t + 1) * TOK)
            outs = []
            for g in range(2):
                h = 4 * g + i
                s = scores_of(of_head(q_ref[i, rows, :], g, low), k_s[...])
                m = jnp.max(s, axis=1, keepdims=True)
                p = jnp.exp(s - m).astype(BF16)
                o = jnp.dot(p, v_s[...], preferred_element_type=F32)
                outs.append(o[:, :128])
                sides[t] = jnp.where(lane == 2 * h, o[:, 128:129], jnp.where(lane == 2 * h + 1, m, sides[t]))
            o_s[i, rows, :] = jnp.where(low, outs[0], outs[1])
        copies.append(pltpu.make_async_copy(o_s.at[i], o_out.at[i], sems.at[i]))
        copies[-1].start()
    for t in range(2):
        ml_s[t * TOK : (t + 1) * TOK, :] = sides[t]
    copies.append(pltpu.make_async_copy(ml_s, ml_out, sems.at[4]))
    copies[-1].start()
    for copy in copies:
        copy.wait()


def near(place, kv, prev, nxt, q):
    return pl.pallas_call(
        near_kernel,
        out_shape=(
            jax.ShapeDtypeStruct((4, BLOCK, 128), F32),
            jax.ShapeDtypeStruct((BLOCK, 128), F32),
        ),
        in_specs=[smem_spec()] + [vmem_spec()] * 4,
        out_specs=(hbm_spec(),) * 2,
        scratch_shapes=[
            VMEM((4, BLOCK, 128), F32),
            VMEM((BLOCK, 128), F32),
            VMEM((3 * BLOCK, 128), BF16),
            VMEM((3 * BLOCK, 256), BF16),
            pltpu.SemaphoreType.DMA((5,)),
        ],
        compiler_params=params(52.5),
        cost_estimate=cost(3 * BLOCK, 8),
    )(place, kv, prev, nxt, q)


def far_kernel(
    got_ref, o_hbm, ml_hbm, q_hbm, keep_hbm, mine_ref, theirs_ref,
    o_s, ml_s, q_s, keep_ref, y_s, k_s, v_s, peak_s, sems,
):
    keep_copy = pltpu.make_async_copy(keep_hbm, keep_ref, sems.at[0])
    ml_copy = pltpu.make_async_copy(ml_hbm, ml_s, sems.at[1])
    q_copies = [pltpu.make_async_copy(q_hbm.at[i], q_s.at[i], sems.at[2 + i]) for i in range(4)]
    o_copies = [pltpu.make_async_copy(o_hbm.at[i], o_s.at[i], sems.at[6 + i]) for i in range(4)]
    for copy in [keep_copy, q_copies[0], ml_copy, o_copies[0]] + q_copies[1:] + o_copies[1:]:
        copy.start()
    k_s[0:NFINE, :] = got_ref[:, 0, 64:80].reshape(NFINE, 128)
    k_s[NFINE:, :] = got_ref[:, 0, 0:64].reshape(NCOARSE, 128)
    keep_copy.wait()
    keep = keep_ref[...]
    v_s[0:NFINE, :128] = got_ref[:, 1, 64:80].reshape(NFINE, 128) * keep[0:NFINE]
    v_s[NFINE:, :128] = got_ref[:, 1, 0:64].reshape(NCOARSE, 128) * keep[NFINE:]
    v_s[:, 128:] = first_lane(NFAR) * keep
    ml_copy.wait()
    low = is_low(TOK)
    top = jnp.full((8, 128), -1e30, F32)
    for i in range(4):
        q_copies[i].wait()
        o_copies[i].wait()
        for t in range(2):
            rows = slice(t * TOK, (t + 1) * TOK)
            outs = []
            for g in range(2):
                h = 4 * g + i
                m = ml_s[rows, 2 * h + 1 : 2 * h + 2]
                d = scores_of(of_head(q_s[i, rows, :], g, low), k_s[...]) - m
                tile = jnp.max(d.reshape(TOK // 8, 8, NFAR), axis=0)
                top = jnp.maximum(top, jnp.max(tile.reshape(8, NFAR // 128, 128), axis=1))
                p = jnp.exp(d).astype(BF16)
                o = jnp.dot(p, v_s[...], preferred_element_type=F32)
                total = o[:, 128:129] + ml_s[rows, 2 * h : 2 * h + 1]
                outs.append((o[:, :128] + o_s[i, rows, :]) * (1.0 / total))
            y_s[i, rows, :] = jnp.where(low, outs[0], outs[1])
    peak_s[...] = top

    @pl.when(jnp.max(peak_s[...]) > LIMIT)
    def _():
        for i in range(4):

            @pl.loop(0, BLOCK // 64)
            def _(t, i=i):
                rows = pl.ds(pl.multiple_of(t * 64, 64), 64)
                low = is_low(64)
                counted = scores_of(jnp.ones((64, 128), BF16), v_s[:, 128:]) > 0
                outs = []
                for g in range(2):
                    h = 4 * g + i
                    s = scores_of(of_head(q_s[i, rows, :], g, low), k_s[...])
                    s = jnp.where(counted, s, -1e30)
                    old = ml_s[rows, 2 * h + 1 : 2 * h + 2]
                    m = jnp.maximum(jnp.max(s, axis=1, keepdims=True), old)
                    p = jnp.exp(s - m).astype(BF16)
                    o = jnp.dot(p, v_s[...], preferred_element_type=F32)
                    shrink = jnp.exp(old - m)
                    total = o[:, 128:129] + ml_s[rows, 2 * h : 2 * h + 1] * shrink
                    outs.append((o[:, :128] + o_s[i, rows, :] * shrink) * (1.0 / total))
                y_s[i, rows, :] = jnp.where(low, outs[0], outs[1])

    for ref, at in ((mine_ref, 0), (theirs_ref, TOK)):
        y = [y_s[i, at : at + TOK, :] for i in range(4)]
        for j in range(2):
            left = jnp.where(low, y[2 * j], swapped(y[2 * j + 1]))
            right = jnp.where(low, swapped(y[2 * j]), y[2 * j + 1])
            ref[:, j * 128 : (j + 1) * 128] = left.astype(BF16)
            ref[:, (j + 2) * 128 : (j + 3) * 128] = right.astype(BF16)


def far(got, o, ml, q, keep):
    return pl.pallas_call(
        far_kernel,
        out_shape=(jax.ShapeDtypeStruct((TOK, HALF), BF16),) * 2,
        in_specs=[vmem_spec()] + [hbm_spec()] * 4,
        out_specs=(vmem_spec(),) * 2,
        scratch_shapes=[
            VMEM((4, BLOCK, 128), F32),
            VMEM((BLOCK, 128), F32),
            VMEM((4, BLOCK, 128), BF16),
            VMEM((NFAR, 128), BF16),
            VMEM((4, BLOCK, 128), F32),
            VMEM((NFAR, 128), BF16),
            VMEM((NFAR, 256), BF16),
            VMEM((8, 128), F32),
            pltpu.SemaphoreType.DMA((10,)),
        ],
        compiler_params=params(51),
        cost_estimate=cost(NFAR),
    )(got, o, ml, q, keep)


def pack_kernel(z_ref, fine_ref, out_ref):
    row = lax.broadcasted_iota(jnp.int32, (256, 256), 0)
    col = lax.broadcasted_iota(jnp.int32, (256, 256), 1)
    part = ((row // 64) % 2) * 2 + row // 128
    source = ((row % 64) // 2) * 8 + part * 2 + row % 2
    pick = jnp.where(col == source, 1.0, 0.0).astype(BF16)
    rows = jnp.dot(pick, z_ref[...].reshape(256, 128), preferred_element_type=F32).astype(BF16)
    for core in range(2):
        for kv in range(2):
            at = core * 128 + kv * 64
            both = jnp.concatenate([rows[at : at + 64], fine_ref[kv * 2 + core]], axis=0)
            for chip in range(8):
                out_ref[chip * 2 + core, kv] = both


def pack(z_rows, fine):
    return pl.pallas_call(
        pack_kernel,
        out_shape=jax.ShapeDtypeStruct((INNERS, 2, 80, 128), BF16),
        in_specs=[vmem_spec()] * 2,
        out_specs=vmem_spec(),
        compiler_params=params(),
    )(z_rows, fine)


def norm_kernel(core_ref, mine_ref, got_ref, gain_ref, out_ref):
    first = core_ref[0] == 0
    mine = mine_ref[...].astype(F32)
    got = got_ref[...].astype(F32)
    total = jnp.sum(mine * mine, axis=1, keepdims=True) + jnp.sum(got * got, axis=1, keepdims=True)
    scale = lax.rsqrt(total / D + EPSILON)
    left = jnp.where(first, mine, got)
    right = jnp.where(first, got, mine)
    out_ref[:, :HALF] = (left * scale * gain_ref[:, :HALF]).astype(BF16)
    out_ref[:, HALF:] = (right * scale * gain_ref[:, HALF:]).astype(BF16)


def finish(core, mine, got, gain):
    return pl.pallas_call(
        norm_kernel,
        out_shape=jax.ShapeDtypeStruct((TOK, D), BF16),
        in_specs=[smem_spec()] + [vmem_spec()] * 3,
        out_specs=vmem_spec(),
        compiler_params=params(),
    )(core, mine, got, gain)


def local(queries, keys, values, pool_fine, pool_coarse, gain):
    core = lax.axis_index("c").reshape(1).astype(jnp.int32)
    group = lax.axis_index(("o0", "z"))
    block = group * 8 + lax.axis_index(("y", "xl"))
    n_blocks = lax.axis_size(ALL) // 2
    place = jnp.stack([group, block, block > 0, block < n_blocks - 1]).astype(jnp.int32)
    fine, coarse, send, qm, kvm = begin(core, queries, keys, values, pool_fine, pool_coarse)
    z_rows = lax.all_to_all(coarse, OUTER, split_axis=0, concat_axis=0, tiled=True)

    got = lax.ppermute(send, "c", [(0, 1), (1, 0)])
    kv = jnp.concatenate([kvm, got[:, :256]], axis=0)
    n = 512
    prev = lax.ppermute(kv, ALL, [(i, i + 2) for i in range(n - 2)])
    nxt = lax.ppermute(kv, ALL, [(i + 2, i) for i in range(n - 2)])
    q, keep = prep(place, qm, got)
    z_rows, q, keep = lax.optimization_barrier((z_rows, q, keep))
    plane = pack(z_rows[:, :8], fine)
    summary = lax.all_to_all(plane, INNER, split_axis=0, concat_axis=0, tiled=True)
    o, ml = near(place, kv, prev, nxt, q)
    mine, theirs = far(summary, o, ml, q, keep)
    back = lax.ppermute(theirs, "c", [(0, 1), (1, 0)])
    return finish(core, mine, back, gain.reshape(1, D))


def solution(mesh):
    torus = Mesh(mesh.devices.reshape(2, ZN, 4, 2, 2), ALL)
    spec = P(ALL, None)
    return jax.shard_map(
        local,
        mesh=torus,
        in_specs=(spec, spec, spec, P(), P(), P()),
        out_specs=spec,
        check_vma=False,
    )
```

time: 187 us -> 103 us (0.55)
  the two profiles are of different devices: /device:TPU:12 before, /device:TPU:83 now
where the time goes in v1:
time: 103 us
  starting transfers between devices  72.2 us (70%)
  Pallas kernels  23.8 us (23%)
  waiting for transfers between devices  4.92 us (5%)
  local copies, waits for them, and re-layouts  1.7 us (2%)
    ppermute x1, starting transfers between devices, local(): back = lax.ppermute(theirs, 'c', [(0, 1), (1, 0)])  40.6 us
    all_to_all x1, starting transfers between devices, local(): lax.all_to_all(coarse, OUTER, split_axis=0, concat_axis=0, tiled=True)  15.9 us
    pallas_call x1, Pallas kernels, near(): pl.pallas_call(near_kernel, out_shape=(jax.ShapeDtypeStruct((4, BLOCK, 12...  9.73 us
    pallas_call x1, Pallas kernels, far(): pl.pallas_call(far_kernel, out_shape=(jax.ShapeDtypeStruct((TOK, HALF), B...  8.48 us
    all_to_all x1, starting transfers between devices, local(): lax.all_to_all(plane, INNER, split_axis=0, concat_axis=0, tiled=True)  6.8 us
    all_to_all x1, waiting for transfers between devices, local(): lax.all_to_all(coarse, OUTER, split_axis=0, concat_axis=0, tiled=True)  3.77 us
    ppermute x1, starting transfers between devices, local(): nxt = lax.ppermute(kv, ALL, [(i + 2, i) for i in range(n - 2)])  3.19 us
    ppermute x1, starting transfers between devices, local(): prev = lax.ppermute(kv, ALL, [(i, i + 2) for i in range(n - 2)])  3.12 us
  transfers between devices with their start and end apart: 6, of which 2 were waited for; matrix products, arithmetic and copies ran while one was open for 0% of the time, Pallas kernels for 12%

profile of v1, /device:TPU:83, one launch (start us, length us, event | category | flops | bytes accessed | tf_op | source)
XLA Modules:
  0.0 102.8 jit_solution(17427277164981528359)
XLA Ops:
  0.0 2.2 %shard_map.64 = (bf16[4,16,128]{2,1,0:T(8,128)(2,1)}, bf16[32,8,128]{2,1,0:T(8,128)(2,1)}, bf16[256,768]{1,0:T(8,128)(2,1)}, bf16[256,512]{1,0:T(8,128)(2,1)}, bf16[256,256]{1,0:T(8,128)(2,1)}) custom-call(s32[1]{0:T(128)} %bitcast.core_ref, bf16[256,1024]{1,0:T(8,128)(2,1)} %q_hbm.1, bf16[256,256]{1,0:T(8,128)(2,1)} %k_hbm.1, bf16[256,256]{1,0:T(8,128)(2,1)} %v_hbm.1, ...), custom_call_target="tpu_custom_call" | custom-call | tf_op jit(solution)/shard_map/pallas_call | solution.py:93
  2.2 2.6 %collective-permute-start = (bf16[256,768]{1,0:T(8,128)(2,1)}, bf16[256,768]{1,0:T(8,128)(2,1)S(1)}, u32[]{:S(2)}, u32[]{:S(2)}) collective-permute-start(bf16[256,768]{1,0:T(8,128)(2,1)} %get-tuple-element.21), channel_id=1, source_target_pairs={{0,1},{1,0},{2,3},{3,2},{4,5},{5,4},{6,7},{7,6},{8,9},{9,8},{10,11... | collective-permute-start | bytes 1179656 | tf_op jit(solution)/shard_map/ppermute | solution.py:409
  4.8 15.9 %all-to-all-start = ((bf16[32,8,128]{2,1,0:T(8,128)(2,1)}), bf16[32,8,128]{2,1,0:T(8,128)(2,1)S(1)}, u32[]{:S(2)}, u32[]{:S(2)}) async-start(bf16[32,8,128]{2,1,0:T(8,128)(2,1)} %get-tuple-element.19), calls=%async_computation | async-start | bytes 131072 | tf_op jit(solution)/shard_map/all_to_all | solution.py:407
  20.7 0.1 pad_add_fusion.place_ref
  20.8 0.0 copy-start.5
  20.8 0.0 collective-permute-done.got_ref
  20.8 0.9 copy-done.5
  21.7 0.0 copy-start.2
  21.7 3.2 %collective-permute-start.2 = (bf16[512,256]{1,0:T(8,128)(2,1)S(1)}, bf16[512,256]{1,0:T(8,128)(2,1)S(1)}, u32[]{:S(2)}, u32[]{:S(2)}) collective-permute-start(bf16[512,256]{1,0:T(8,128)(2,1)S(1)} %pad_maximum_fusion.kv_ref), channel_id=1, source_target_pairs={{2,0},{3,1},{4,2},{5,3},{6,4},{7,5},{8,6},{9,7},{10,8},{11,9},{12,... | collective-permute-start | bytes 786440 | tf_op jit(solution)/shard_map/ppermute | solution.py:413
  24.9 3.1 %collective-permute-start.1 = (bf16[512,256]{1,0:T(8,128)(2,1)S(1)}, bf16[512,256]{1,0:T(8,128)(2,1)S(1)}, u32[]{:S(2)}, u32[]{:S(2)}) collective-permute-start(bf16[512,256]{1,0:T(8,128)(2,1)S(1)} %pad_maximum_fusion.kv_ref), channel_id=1, source_target_pairs={{0,2},{1,3},{2,4},{3,5},{4,6},{5,7},{6,8},{7,9},{8,10},{9,11},{10,... | collective-permute-start | bytes 786440 | tf_op jit(solution)/shard_map/ppermute | solution.py:412
  28.1 0.0 copy-done.2
  28.1 0.0 copy-start
  28.1 1.2 %shard_map.65 = (bf16[4,512,128]{2,1,0:T(8,128)(2,1)S(1)}, bf16[1280,128]{1,0:T(8,128)(2,1)S(1)}) custom-call(s32[4]{0:T(128)S(1)} %pad_add_fusion.place_ref, bf16[256,512]{1,0:T(8,128)(2,1)S(1)} %copy-done.2, bf16[256,768]{1,0:T(8,128)(2,1)S(1)} %collective-permute-done.got_ref), custom_call_target="tpu_custom_call" | custom-call | flops 3221225472 | bytes 4194304 | tf_op jit(solution)/shard_map/pallas_call | solution.py:175
  29.3 0.0 copy-start.3
  29.3 0.8 copy-done.3
  30.1 3.8 %all-to-all-done.z_ref = bf16[32,8,128]{2,1,0:T(8,128)(2,1)S(1)} async-done(((bf16[32,8,128]{2,1,0:T(8,128)(2,1)}), bf16[32,8,128]{2,1,0:T(8,128)(2,1)S(1)}, u32[]{:S(2)}, u32[]{:S(2)}) %all-to-all-start) | async-done | bytes 65568 | tf_op jit(solution)/shard_map/all_to_all | solution.py:407
  33.9 0.0 copy-done
  33.9 1.1 %shard_map.66 = bf16[16,2,80,128]{3,2,1,0:T(8,128)(2,1)} custom-call(bf16[32,8,128]{2,1,0:T(8,128)(2,1)S(1)} %all-to-all-done.z_ref, bf16[4,16,128]{2,1,0:T(8,128)(2,1)S(1)} %copy-done), custom_call_target="tpu_custom_call" | custom-call | tf_op jit(solution)/shard_map/pallas_call | solution.py:369
  34.9 6.8 %all-to-all-start.1 = ((bf16[16,2,80,128]{3,2,1,0:T(8,128)(2,1)}), bf16[16,2,80,128]{3,2,1,0:T(8,128)(2,1)S(1)}, u32[]{:S(2)}, u32[]{:S(2)}) async-start(bf16[16,2,80,128]{3,2,1,0:T(8,128)(2,1)} %shard_map.66), calls=%async_computation.1 | async-start | bytes 1310720 | tf_op jit(solution)/shard_map/all_to_all | solution.py:417
  41.7 0.0 copy-start.4
  41.7 0.0 collective-permute-done.2.next_ref
  41.8 0.0 collective-permute-done.1.prev_ref
  41.8 9.7 %shard_map.67 = (f32[4,512,128]{2,1,0:T(8,128)}, f32[512,128]{1,0:T(8,128)S(1)}) custom-call(s32[4]{0:T(128)S(1)} %pad_add_fusion.place_ref, bf16[512,256]{1,0:T(8,128)(2,1)S(1)} %pad_maximum_fusion.kv_ref, bf16[512,256]{1,0:T(8,128)(2,1)S(1)} %collective-permute-done.1.prev_ref, bf16[512,256]{1,0:T(8,128)(2,1)S(1)} %collective-permute-done.2.next_ref, ...), custom_call_target="tpu_custom_call" | custom-call | flops 25769803776 | bytes 4194304 | tf_op jit(solution)/shard_map/pallas_call | solution.py:240
  51.5 0.0 all-to-all-done.1.got_ref
  51.5 0.0 copy-done.4
  51.5 8.5 %shard_map.68 = (bf16[256,512]{1,0:T(8,128)(2,1)S(1)}, bf16[256,512]{1,0:T(8,128)(2,1)S(1)}) custom-call(bf16[16,2,80,128]{3,2,1,0:T(8,128)(2,1)S(1)} %all-to-all-done.1.got_ref, f32[4,512,128]{2,1,0:T(8,128)} %get-tuple-element.28.o_hbm, f32[512,128]{1,0:T(8,128)S(1)} %get-tuple-element.29.ml_hbm, bf16[4,512,128]{2,1,0:T(8,128)(2,1)S(1)} %copy-done.4, ...), custom_call_target="tpu_custom_call" | custom-call | flops 2684354560 | bytes 4194304 | tf_op jit(solution)/shard_map/pallas_call | solution.py:332
  60.0 0.0 copy-start.1
  60.0 40.6 %collective-permute-start.3 = (bf16[256,512]{1,0:T(8,128)(2,1)S(1)}, bf16[256,512]{1,0:T(8,128)(2,1)S(1)}, u32[]{:S(2)}, u32[]{:S(2)}) collective-permute-start(bf16[256,512]{1,0:T(8,128)(2,1)S(1)} %get-tuple-element.32), channel_id=1, source_target_pairs={{0,1},{1,0},{2,3},{3,2},{4,5},{5,4},{6,7},{7,6},{8,9},{9,8},{10,11... | collective-permute-start | bytes 786440 | tf_op jit(solution)/shard_map/ppermute | solution.py:420
  100.6 1.1 %collective-permute-done.3.got_ref = bf16[256,512]{1,0:T(8,128)(2,1)S(1)} collective-permute-done((bf16[256,512]{1,0:T(8,128)(2,1)S(1)}, bf16[256,512]{1,0:T(8,128)(2,1)S(1)}, u32[]{:S(2)}, u32[]{:S(2)}) %collective-permute-start.3) | collective-permute-done | bytes 262176 | tf_op jit(solution)/shard_map/ppermute | solution.py:420
  101.8 0.0 copy-done.1
  101.8 1.1 %shard_map.69 = bf16[256,1024]{1,0:T(8,128)(2,1)} custom-call(s32[1]{0:T(128)} %bitcast.core_ref, bf16[256,512]{1,0:T(8,128)(2,1)S(1)} %get-tuple-element.31.mine_ref, bf16[256,512]{1,0:T(8,128)(2,1)S(1)} %collective-permute-done.3.got_ref, f32[1,1024]{1,0:T(1,128)S(1)} %bitcast.7), custom_call_target="tpu_custom_call" | custom-call | tf_op jit(solution)/shard_map/pallas_call | solution.py:391
  (2 shorter events, 0.0 us)
Async XLA Ops:
  2.2 18.6 %collective-permute-start = (bf16[256,768]{1,0:T(8,128)(2,1)}, bf16[256,768]{1,0:T(8,128)(2,1)S(1)}, u32[]{:S(2)}, u32[]{:S(2)}) collective-permute-start(bf16[256,768]{1,0:T(8,128)(2,1)} %get-tuple-element.21), channel_id=1, source_target_pairs={{0,1},{1,0},{2,3},{3,2},{4,5},{5,4},{6,7},{7,6},{8,9},{9,8},{10,11... | collective-permute-start | bytes 1179656 | tf_op jit(solution)/shard_map/ppermute | solution.py:409
  4.8 29.1 %all-to-all-start = ((bf16[32,8,128]{2,1,0:T(8,128)(2,1)}), bf16[32,8,128]{2,1,0:T(8,128)(2,1)S(1)}, u32[]{:S(2)}, u32[]{:S(2)}) async-start(bf16[32,8,128]{2,1,0:T(8,128)(2,1)} %get-tuple-element.19), calls=%async_computation | async-start | bytes 131072 | tf_op jit(solution)/shard_map/all_to_all | solution.py:407
  20.8 0.9 copy-start.5
  21.7 6.4 %copy-start.2 = (bf16[256,512]{1,0:T(8,128)(2,1)S(1)}, bf16[256,512]{1,0:T(8,128)(2,1)}, u32[]{:S(2)}) copy-start(bf16[256,512]{1,0:T(8,128)(2,1)} %get-tuple-element.20.qm_ref) | copy-start | bytes 786436
  21.7 20.0 %collective-permute-start.2 = (bf16[512,256]{1,0:T(8,128)(2,1)S(1)}, bf16[512,256]{1,0:T(8,128)(2,1)S(1)}, u32[]{:S(2)}, u32[]{:S(2)}) collective-permute-start(bf16[512,256]{1,0:T(8,128)(2,1)S(1)} %pad_maximum_fusion.kv_ref), channel_id=1, source_target_pairs={{2,0},{3,1},{4,2},{5,3},{6,4},{7,5},{8,6},{9,7},{10,8},{11,9},{12,... | collective-permute-start | bytes 786440 | tf_op jit(solution)/shard_map/ppermute | solution.py:413
  24.9 16.8 %collective-permute-start.1 = (bf16[512,256]{1,0:T(8,128)(2,1)S(1)}, bf16[512,256]{1,0:T(8,128)(2,1)S(1)}, u32[]{:S(2)}, u32[]{:S(2)}) collective-permute-start(bf16[512,256]{1,0:T(8,128)(2,1)S(1)} %pad_maximum_fusion.kv_ref), channel_id=1, source_target_pairs={{0,2},{1,3},{2,4},{3,5},{4,6},{5,7},{6,8},{7,9},{8,10},{9,11},{10,... | collective-permute-start | bytes 786440 | tf_op jit(solution)/shard_map/ppermute | solution.py:412
  28.1 5.8 %copy-start = (bf16[4,16,128]{2,1,0:T(8,128)(2,1)S(1)}, bf16[4,16,128]{2,1,0:T(8,128)(2,1)}, u32[]{:S(2)}) copy-start(bf16[4,16,128]{2,1,0:T(8,128)(2,1)} %get-tuple-element.25.fine_ref) | copy-start | bytes 49156
  29.3 0.8 copy-start.3
  34.9 16.6 %all-to-all-start.1 = ((bf16[16,2,80,128]{3,2,1,0:T(8,128)(2,1)}), bf16[16,2,80,128]{3,2,1,0:T(8,128)(2,1)S(1)}, u32[]{:S(2)}, u32[]{:S(2)}) async-start(bf16[16,2,80,128]{3,2,1,0:T(8,128)(2,1)} %shard_map.66), calls=%async_computation.1 | async-start | bytes 1310720 | tf_op jit(solution)/shard_map/all_to_all | solution.py:417
  41.7 9.8 %copy-start.4 = (bf16[4,512,128]{2,1,0:T(8,128)(2,1)S(1)}, bf16[4,512,128]{2,1,0:T(8,128)(2,1)}, u32[]{:S(2)}) copy-start(bf16[4,512,128]{2,1,0:T(8,128)(2,1)} %copy-done.3) | copy-start | bytes 1572868
  60.0 41.8 %copy-start.1 = (f32[1024]{0:T(1024)S(1)}, f32[1024]{0:T(1024)}, u32[]{:S(2)}) copy-start(f32[1024]{0:T(1024)} %param.11) | copy-start | bytes 12292
  60.0 41.7 %collective-permute-start.3 = (bf16[256,512]{1,0:T(8,128)(2,1)S(1)}, bf16[256,512]{1,0:T(8,128)(2,1)S(1)}, u32[]{:S(2)}, u32[]{:S(2)}) collective-permute-start(bf16[256,512]{1,0:T(8,128)(2,1)S(1)} %get-tuple-element.32), channel_id=1, source_target_pairs={{0,1},{1,0},{2,3},{3,2},{4,5},{5,4},{6,7},{7,6},{8,9},{9,8},{10,11... | collective-permute-start | bytes 786440 | tf_op jit(solution)/shard_map/ppermute | solution.py:420

commit v2 on v1

--- a/solution.py
+++ b/solution.py
@@ -55,15 +55,16 @@
 
 
 def begin_kernel(
-    core_ref, q_hbm, k_hbm, v_hbm, wf_hbm, wc_hbm, fine_ref, coarse_ref, send_ref, qm_ref, kvm_ref, k_s, v_s, wf_s, wc_s, sems
+    core_ref, q_hbm, k_hbm, v_hbm, wf_hbm, wc_hbm, fine_ref, coarse_ref, send_ref, kvm_ref, k_s, v_s, wf_s, wc_s, sems
 ):
     pairs = [(wf_hbm, wf_s), (wc_hbm, wc_s), (k_hbm, k_s), (v_hbm, v_s)]
     mine = core_ref[0]
     for src, width, at in ((q_hbm, HALF, 256), (k_hbm, 128, 0), (v_hbm, 128, 128)):
-        for which, dst in ((1 - mine, send_ref), (mine, kvm_ref if width == 128 else qm_ref)):
+        for which, dst in ((1 - mine, send_ref), (mine, kvm_ref)):
+            if width == HALF and dst is kvm_ref:
+                continue
             cols = pl.ds(pl.multiple_of(which * width, 128), width)
-            start = 0 if dst is qm_ref else at
-            pairs.append((src.at[:, cols], dst.at[:, start : start + width]))
+            pairs.append((src.at[:, cols], dst.at[:, at : at + width]))
     copies = [pltpu.make_async_copy(src, dst, sems.at[i]) for i, (src, dst) in enumerate(pairs)]
     for copy in copies:
         copy.start()
@@ -96,25 +97,23 @@
             jax.ShapeDtypeStruct((4, TOK // FINE, 128), BF16),
             jax.ShapeDtypeStruct((GROUPS, ZROWS, 128), BF16),
             jax.ShapeDtypeStruct((TOK, 768), BF16),
-            jax.ShapeDtypeStruct((TOK, HALF), BF16),
             jax.ShapeDtypeStruct((TOK, 256), BF16),
         ),
         in_specs=[smem_spec()] + [hbm_spec()] * 5,
-        out_specs=(vmem_spec(),) * 5,
+        out_specs=(vmem_spec(),) * 4,
         scratch_shapes=[
             VMEM((TOK, 256), BF16),
             VMEM((TOK, 256), BF16),
             VMEM((2 * KVH, FINE), F32),
             VMEM((RATIO, 2 * KVH), F32),
-            pltpu.SemaphoreType.DMA((10,)),
+            pltpu.SemaphoreType.DMA((9,)),
         ],
         compiler_params=params(54),
     )(core, queries, keys, values, pool_fine.T, pool_coarse)
 
 
-NFINE = 256
-NCOARSE = 1024
-NFAR = NFINE + NCOARSE
+MESSAGE = 80
+NFAR = INNERS * MESSAGE
 LIMIT = 40.0
 
 
@@ -143,26 +142,25 @@
     return jnp.where(one, 1.0, 0.0).astype(BF16)
 
 
-def fine_keep(group, block):
-    row = lax.broadcasted_iota(jnp.int32, (NFINE, 128), 0)
-    src_block = group * 8 + row // 32
-    return jnp.abs(src_block - block) > 1
-
-
-def coarse_keep(group, block):
-    row = lax.broadcasted_iota(jnp.int32, (NCOARSE, 128), 0)
-    src_group = (row // 2) % GROUPS
-    src_block = src_group * 8 + row // 128
-    return (src_group != group) & (jnp.abs(src_block - block) > 1)
-
-
-def prep_kernel(place_ref, qm_ref, got_ref, q_ref, keep_ref):
-    group = place_ref[0]
-    block = place_ref[1]
-    keep_ref[0:NFINE, :] = jnp.where(fine_keep(group, block), 1.0, 0.0).astype(BF16)
-    keep_ref[NFINE:, :] = jnp.where(coarse_keep(group, block), 1.0, 0.0).astype(BF16)
+def counted_rows(group, block):
+    source = lax.broadcasted_iota(jnp.int32, (INNERS, MESSAGE, 128), 0)
+    row = lax.broadcasted_iota(jnp.int32, (INNERS, MESSAGE, 128), 1)
+    coarse = row < 2 * GROUPS
+    src_group = jnp.where(coarse, row // 2, group)
+    src_block = src_group * 8 + source // 2
+    far_off = jnp.abs(src_block - block) > 1
+    keep = far_off & (jnp.logical_not(coarse) | (src_group != group))
+    return jnp.where(keep, 1.0, 0.0).reshape(NFAR, 128).astype(BF16)
+
+
+def prep_kernel(place_ref, q_hbm, got_ref, q_ref, qm_ref, sem):
+    cols = pl.ds(pl.multiple_of(place_ref[4] * HALF, 128), HALF)
+    copy = pltpu.make_async_copy(q_hbm.at[:, cols], qm_ref, sem)
+    copy.start()
     low = is_low(TOK)
-    for ref, first, at in ((qm_ref, 0, 0), (got_ref, 256, TOK)):
+    for ref, first, at in ((got_ref, 256, TOK), (qm_ref, 0, 0)):
+        if ref is qm_ref:
+            copy.wait()
         pairs = [ref[:, first + j * 128 : first + (j + 1) * 128].astype(F32) * HD ** (-0.5) for j in range(4)]
         other = [swapped(x) for x in pairs]
         for j in range(2):
@@ -171,18 +169,16 @@
             q_ref[2 * j + 1, rows, :] = jnp.where(low, other[j], pairs[j + 2]).astype(BF16)
 
 
-def prep(place, qm, got):
+def prep(place, queries, got):
     return pl.pallas_call(
         prep_kernel,
-        out_shape=(
-            jax.ShapeDtypeStruct((4, BLOCK, 128), BF16),
-            jax.ShapeDtypeStruct((NFAR, 128), BF16),
-        ),
-        in_specs=[smem_spec()] + [vmem_spec()] * 2,
-        out_specs=(vmem_spec(), vmem_spec()),
+        out_shape=jax.ShapeDtypeStruct((4, BLOCK, 128), BF16),
+        in_specs=[smem_spec(), hbm_spec(), vmem_spec()],
+        out_specs=vmem_spec(),
+        scratch_shapes=[VMEM((TOK, HALF), BF16), pltpu.SemaphoreType.DMA],
         compiler_params=params(),
         cost_estimate=cost(3 * BLOCK),
-    )(place, qm, got)
+    )(place, queries, got)
 
 
 def of_head(pair, g, low):
@@ -190,7 +186,7 @@
     return jnp.where(low, pair, zero) if g == 0 else jnp.where(low, zero, pair)
 
 
-def near_kernel(place_ref, kv_ref, prev_ref, next_ref, q_ref, o_out, ml_out, o_s, ml_s, k_s, v_s, sems):
+def near_kernel(place_ref, kv_ref, prev_ref, next_ref, q_ref, o_s, ml_s, k_s, v_s):
     k_s[0:BLOCK, :] = kv_ref[:, :128]
     v_s[0:BLOCK, :128] = kv_ref[:, 128:]
     v_s[0:BLOCK, 128:] = first_lane(BLOCK)
@@ -211,7 +207,6 @@
 
     low = is_low(TOK)
     lane = lax.broadcasted_iota(jnp.int32, (TOK, 128), 1)
-    copies = []
     sides = [jnp.zeros((TOK, 128), F32)] * 2
     for i in range(4):
         for t in range(2):
@@ -225,78 +220,58 @@
                 o = jnp.dot(p, v_s[...], preferred_element_type=F32)
                 outs.append(o[:, :128])
                 sides[t] = jnp.where(lane == 2 * h, o[:, 128:129], jnp.where(lane == 2 * h + 1, m, sides[t]))
-            o_s[i, rows, :] = jnp.where(low, outs[0], outs[1])
-        copies.append(pltpu.make_async_copy(o_s.at[i], o_out.at[i], sems.at[i]))
-        copies[-1].start()
+            o_s[i, rows, :] = jnp.where(low, outs[0], outs[1]).astype(BF16)
     for t in range(2):
         ml_s[t * TOK : (t + 1) * TOK, :] = sides[t]
-    copies.append(pltpu.make_async_copy(ml_s, ml_out, sems.at[4]))
-    copies[-1].start()
-    for copy in copies:
-        copy.wait()
 
 
 def near(place, kv, prev, nxt, q):
     return pl.pallas_call(
         near_kernel,
         out_shape=(
-            jax.ShapeDtypeStruct((4, BLOCK, 128), F32),
+            jax.ShapeDtypeStruct((4, BLOCK, 128), BF16),
             jax.ShapeDtypeStruct((BLOCK, 128), F32),
         ),
         in_specs=[smem_spec()] + [vmem_spec()] * 4,
-        out_specs=(hbm_spec(),) * 2,
+        out_specs=(vmem_spec(),) * 2,
         scratch_shapes=[
-            VMEM((4, BLOCK, 128), F32),
-            VMEM((BLOCK, 128), F32),
             VMEM((3 * BLOCK, 128), BF16),
             VMEM((3 * BLOCK, 256), BF16),
-            pltpu.SemaphoreType.DMA((5,)),
         ],
-        compiler_params=params(52.5),
+        compiler_params=params(48),
         cost_estimate=cost(3 * BLOCK, 8),
     )(place, kv, prev, nxt, q)
 
 
 def far_kernel(
-    got_ref, o_hbm, ml_hbm, q_hbm, keep_hbm, mine_ref, theirs_ref,
-    o_s, ml_s, q_s, keep_ref, y_s, k_s, v_s, peak_s, sems,
+    place_ref, got_ref, o_s, ml_s, q_s, mine_ref, theirs_ref, y_s, v_s, peak_s
 ):
-    keep_copy = pltpu.make_async_copy(keep_hbm, keep_ref, sems.at[0])
-    ml_copy = pltpu.make_async_copy(ml_hbm, ml_s, sems.at[1])
-    q_copies = [pltpu.make_async_copy(q_hbm.at[i], q_s.at[i], sems.at[2 + i]) for i in range(4)]
-    o_copies = [pltpu.make_async_copy(o_hbm.at[i], o_s.at[i], sems.at[6 + i]) for i in range(4)]
-    for copy in [keep_copy, q_copies[0], ml_copy, o_copies[0]] + q_copies[1:] + o_copies[1:]:
-        copy.start()
-    k_s[0:NFINE, :] = got_ref[:, 0, 64:80].reshape(NFINE, 128)
-    k_s[NFINE:, :] = got_ref[:, 0, 0:64].reshape(NCOARSE, 128)
-    keep_copy.wait()
-    keep = keep_ref[...]
-    v_s[0:NFINE, :128] = got_ref[:, 1, 64:80].reshape(NFINE, 128) * keep[0:NFINE]
-    v_s[NFINE:, :128] = got_ref[:, 1, 0:64].reshape(NCOARSE, 128) * keep[NFINE:]
+    keep = counted_rows(place_ref[0], place_ref[1])
+    k = got_ref[:, 0].reshape(NFAR, 128)
+    v_s[:, :128] = got_ref[:, 1].reshape(NFAR, 128) * keep
     v_s[:, 128:] = first_lane(NFAR) * keep
-    ml_copy.wait()
     low = is_low(TOK)
     top = jnp.full((8, 128), -1e30, F32)
     for i in range(4):
-        q_copies[i].wait()
-        o_copies[i].wait()
         for t in range(2):
             rows = slice(t * TOK, (t + 1) * TOK)
             outs = []
             for g in range(2):
                 h = 4 * g + i
                 m = ml_s[rows, 2 * h + 1 : 2 * h + 2]
-                d = scores_of(of_head(q_s[i, rows, :], g, low), k_s[...]) - m
+                d = scores_of(of_head(q_s[i, rows, :], g, low), k) - m
                 tile = jnp.max(d.reshape(TOK // 8, 8, NFAR), axis=0)
                 top = jnp.maximum(top, jnp.max(tile.reshape(8, NFAR // 128, 128), axis=1))
                 p = jnp.exp(d).astype(BF16)
                 o = jnp.dot(p, v_s[...], preferred_element_type=F32)
                 total = o[:, 128:129] + ml_s[rows, 2 * h : 2 * h + 1]
-                outs.append((o[:, :128] + o_s[i, rows, :]) * (1.0 / total))
+                outs.append((o[:, :128], 1.0 / total))
+            old = o_s[i, rows, :].astype(F32)
+            outs = [(o + old) * scale for o, scale in outs]
             y_s[i, rows, :] = jnp.where(low, outs[0], outs[1])
-    peak_s[...] = top
-
-    @pl.when(jnp.max(peak_s[...]) > LIMIT)
+    peak = top
+
+    @pl.when(jnp.max(peak) > LIMIT)
     def _():
         for i in range(4):
 
@@ -308,7 +283,7 @@
                 outs = []
                 for g in range(2):
                     h = 4 * g + i
-                    s = scores_of(of_head(q_s[i, rows, :], g, low), k_s[...])
+                    s = scores_of(of_head(q_s[i, rows, :], g, low), k)
                     s = jnp.where(counted, s, -1e30)
                     old = ml_s[rows, 2 * h + 1 : 2 * h + 2]
                     m = jnp.maximum(jnp.max(s, axis=1, keepdims=True), old)
@@ -316,7 +291,7 @@
                     o = jnp.dot(p, v_s[...], preferred_element_type=F32)
                     shrink = jnp.exp(old - m)
                     total = o[:, 128:129] + ml_s[rows, 2 * h : 2 * h + 1] * shrink
-                    outs.append((o[:, :128] + o_s[i, rows, :] * shrink) * (1.0 / total))
+                    outs.append((o[:, :128] + o_s[i, rows, :].astype(F32) * shrink) * (1.0 / total))
                 y_s[i, rows, :] = jnp.where(low, outs[0], outs[1])
 
     for ref, at in ((mine_ref, 0), (theirs_ref, TOK)):
@@ -328,26 +303,20 @@
             ref[:, (j + 2) * 128 : (j + 3) * 128] = right.astype(BF16)
 
 
-def far(got, o, ml, q, keep):
+def far(place, got, o, ml, q):
     return pl.pallas_call(
         far_kernel,
         out_shape=(jax.ShapeDtypeStruct((TOK, HALF), BF16),) * 2,
-        in_specs=[vmem_spec()] + [hbm_spec()] * 4,
+        in_specs=[smem_spec()] + [vmem_spec()] * 4,
         out_specs=(vmem_spec(),) * 2,
         scratch_shapes=[
             VMEM((4, BLOCK, 128), F32),
-            VMEM((BLOCK, 128), F32),
-            VMEM((4, BLOCK, 128), BF16),
-            VMEM((NFAR, 128), BF16),
-            VMEM((4, BLOCK, 128), F32),
-            VMEM((NFAR, 128), BF16),
             VMEM((NFAR, 256), BF16),
             VMEM((8, 128), F32),
-            pltpu.SemaphoreType.DMA((10,)),
         ],
-        compiler_params=params(51),
+        compiler_params=params(48),
         cost_estimate=cost(NFAR),
-    )(got, o, ml, q, keep)
+    )(place, got, o, ml, q)
 
 
 def pack_kernel(z_ref, fine_ref, out_ref):
@@ -402,8 +371,8 @@
     group = lax.axis_index(("o0", "z"))
     block = group * 8 + lax.axis_index(("y", "xl"))
     n_blocks = lax.axis_size(ALL) // 2
-    place = jnp.stack([group, block, block > 0, block < n_blocks - 1]).astype(jnp.int32)
-    fine, coarse, send, qm, kvm = begin(core, queries, keys, values, pool_fine, pool_coarse)
+    place = jnp.stack([group, block, block > 0, block < n_blocks - 1, core[0]]).astype(jnp.int32)
+    fine, coarse, send, kvm = begin(core, queries, keys, values, pool_fine, pool_coarse)
     z_rows = lax.all_to_all(coarse, OUTER, split_axis=0, concat_axis=0, tiled=True)
 
     got = lax.ppermute(send, "c", [(0, 1), (1, 0)])
@@ -411,12 +380,12 @@
     n = 512
     prev = lax.ppermute(kv, ALL, [(i, i + 2) for i in range(n - 2)])
     nxt = lax.ppermute(kv, ALL, [(i + 2, i) for i in range(n - 2)])
-    q, keep = prep(place, qm, got)
-    z_rows, q, keep = lax.optimization_barrier((z_rows, q, keep))
+    q = prep(place, queries, got)
+    z_rows, q = lax.optimization_barrier((z_rows, q))
     plane = pack(z_rows[:, :8], fine)
     summary = lax.all_to_all(plane, INNER, split_axis=0, concat_axis=0, tiled=True)
     o, ml = near(place, kv, prev, nxt, q)
-    mine, theirs = far(summary, o, ml, q, keep)
+    mine, theirs = far(place, summary, o, ml, q)
     back = lax.ppermute(theirs, "c", [(0, 1), (1, 0)])
     return finish(core, mine, back, gain.reshape(1, D))
 

time: 103 us -> 69.7 us (0.68)
  the two profiles are of different devices: /device:TPU:83 before, /device:TPU:1 now
where the time goes in v2:
time: 69.7 us; the launch traced here: 69.2 us
  starting transfers between devices  36.2 us (52%)
  Pallas kernels  20.4 us (29%)
  waiting for transfers between devices  11.4 us (16%)
  other arithmetic  0.92 us (1%)
    all_to_all x1, starting transfers between devices, local(): lax.all_to_all(coarse, OUTER, split_axis=0, concat_axis=0, tiled=True)  12.3 us
    ppermute x1, starting transfers between devices, local(): got = lax.ppermute(send, 'c', [(0, 1), (1, 0)])  8.92 us
    pallas_call x1, Pallas kernels, near(): pl.pallas_call(near_kernel, out_shape=(jax.ShapeDtypeStruct((4, BLOCK, 12...  8.48 us
    all_to_all x1, waiting for transfers between devices, local(): lax.all_to_all(coarse, OUTER, split_axis=0, concat_axis=0, tiled=True)  7.52 us
    pallas_call x1, Pallas kernels, far(): pl.pallas_call(far_kernel, out_shape=(jax.ShapeDtypeStruct((TOK, HALF), B...  6.94 us
    all_to_all x1, starting transfers between devices, local(): lax.all_to_all(plane, INNER, split_axis=0, concat_axis=0, tiled=True)  6.62 us
    ppermute x1, starting transfers between devices, local(): prev = lax.ppermute(kv, ALL, [(i, i + 2) for i in range(n - 2)])  4 us
    ppermute x1, starting transfers between devices, local(): back = lax.ppermute(theirs, 'c', [(0, 1), (1, 0)])  3.08 us
  transfers between devices with their start and end apart: 6, of which 3 were waited for; matrix products, arithmetic and copies ran while one was open for 1% of the time, Pallas kernels for 15%

profile of v2, /device:TPU:1, one launch (start us, length us, event | category | flops | bytes accessed | tf_op | source)
XLA Modules:
  0.0 69.2 jit_solution(13904690371195196880)
XLA Ops:
  0.0 2.0 %shard_map.64 = (bf16[4,16,128]{2,1,0:T(8,128)(2,1)}, bf16[32,8,128]{2,1,0:T(8,128)(2,1)}, bf16[256,768]{1,0:T(8,128)(2,1)}, bf16[256,256]{1,0:T(8,128)(2,1)}) custom-call(s32[1]{0:T(128)} %bitcast.core_ref, bf16[256,1024]{1,0:T(8,128)(2,1)} %q_hbm.3, bf16[256,256]{1,0:T(8,128)(2,1)} %k_hbm.1, bf16[256,256]{1,0:T(8,128)(2,1)} %v_hbm.1, f32[8,16]{1,0:T(8,128)} %bitcast.8, ...), custom_call_target="tpu_custom_call" | custom-call | tf_op jit(solution)/shard_map/pallas_call | solution.py:94
  2.0 0.0 copy-start
  2.1 8.9 %collective-permute-start = (bf16[256,768]{1,0:T(8,128)(2,1)}, bf16[256,768]{1,0:T(8,128)(2,1)S(1)}, u32[]{:S(2)}, u32[]{:S(2)}) collective-permute-start(bf16[256,768]{1,0:T(8,128)(2,1)} %get-tuple-element.16), channel_id=1, source_target_pairs={{0,1},{1,0},{2,3},{3,2},{4,5},{5,4},{6,7},{7,6},{8,9},{9,8},{10,11... | collective-permute-start | bytes 1179656 | tf_op jit(solution)/shard_map/ppermute | solution.py:378
  11.0 12.3 %all-to-all-start = ((bf16[32,8,128]{2,1,0:T(8,128)(2,1)}), bf16[32,8,128]{2,1,0:T(8,128)(2,1)S(1)}, u32[]{:S(2)}, u32[]{:S(2)}) async-start(bf16[32,8,128]{2,1,0:T(8,128)(2,1)} %get-tuple-element.15), calls=%async_computation | async-start | bytes 131072 | tf_op jit(solution)/shard_map/all_to_all | solution.py:376
  23.3 0.1 stack.27.place_ref
  23.4 0.0 collective-permute-done.got_ref
  23.4 0.9 %pad_maximum_fusion.kv_ref = bf16[512,256]{1,0:T(8,128)(2,1)S(1)} fusion(bf16[256,256]{1,0:T(8,128)(2,1)S(1)} %slice.4, bf16[256,256]{1,0:T(8,128)(2,1)} %get-tuple-element.19), kind=kLoop, calls=%fused_computation | loop fusion | flops 524288 | bytes 524288 | tf_op jit(solution)/shard_map/concatenate | solution.py:379
  24.3 0.0 copy-start.1
  24.3 1.3 %collective-permute-start.2 = (bf16[512,256]{1,0:T(8,128)(2,1)S(1)}, bf16[512,256]{1,0:T(8,128)(2,1)S(1)}, u32[]{:S(2)}, u32[]{:S(2)}) collective-permute-start(bf16[512,256]{1,0:T(8,128)(2,1)S(1)} %pad_maximum_fusion.kv_ref), channel_id=1, source_target_pairs={{2,0},{3,1},{4,2},{5,3},{6,4},{7,5},{8,6},{9,7},{10,8},{11,9},{12,... | collective-permute-start | bytes 786440 | tf_op jit(solution)/shard_map/ppermute | solution.py:382
  25.6 4.0 %collective-permute-start.1 = (bf16[512,256]{1,0:T(8,128)(2,1)S(1)}, bf16[512,256]{1,0:T(8,128)(2,1)S(1)}, u32[]{:S(2)}, u32[]{:S(2)}) collective-permute-start(bf16[512,256]{1,0:T(8,128)(2,1)S(1)} %pad_maximum_fusion.kv_ref), channel_id=1, source_target_pairs={{0,2},{1,3},{2,4},{3,5},{4,6},{5,7},{6,8},{7,9},{8,10},{9,11},{10,... | collective-permute-start | bytes 786440 | tf_op jit(solution)/shard_map/ppermute | solution.py:381
  29.7 0.0 copy-done
  29.7 0.9 %shard_map.65.q_ref.q_s = bf16[4,512,128]{2,1,0:T(8,128)(2,1)S(1)} custom-call(s32[5]{0:T(128)S(1)} %stack.27.place_ref, bf16[256,1024]{1,0:T(8,128)(2,1)S(1)} %copy-done, bf16[256,768]{1,0:T(8,128)(2,1)S(1)} %collective-permute-done.got_ref), custom_call_target="tpu_custom_call" | custom-call | flops 3221225472 | bytes 4194304 | tf_op jit(solution)/shard_map/pallas_call | solution.py:173
  30.5 7.5 %all-to-all-done.z_ref = bf16[32,8,128]{2,1,0:T(8,128)(2,1)S(1)} async-done(((bf16[32,8,128]{2,1,0:T(8,128)(2,1)}), bf16[32,8,128]{2,1,0:T(8,128)(2,1)S(1)}, u32[]{:S(2)}, u32[]{:S(2)}) %all-to-all-start) | async-done | bytes 65568 | tf_op jit(solution)/shard_map/all_to_all | solution.py:376
  38.1 0.0 copy-done.1
  38.1 1.1 %shard_map.66 = bf16[16,2,80,128]{3,2,1,0:T(8,128)(2,1)} custom-call(bf16[32,8,128]{2,1,0:T(8,128)(2,1)S(1)} %all-to-all-done.z_ref, bf16[4,16,128]{2,1,0:T(8,128)(2,1)S(1)} %copy-done.1), custom_call_target="tpu_custom_call" | custom-call | tf_op jit(solution)/shard_map/pallas_call | solution.py:338
  39.1 6.6 %all-to-all-start.1 = ((bf16[16,2,80,128]{3,2,1,0:T(8,128)(2,1)}), bf16[16,2,80,128]{3,2,1,0:T(8,128)(2,1)S(1)}, u32[]{:S(2)}, u32[]{:S(2)}) async-start(bf16[16,2,80,128]{3,2,1,0:T(8,128)(2,1)} %shard_map.66), calls=%async_computation.1 | async-start | bytes 1310720 | tf_op jit(solution)/shard_map/all_to_all | solution.py:386
  45.7 0.0 collective-permute-done.2.next_ref
  45.7 0.0 collective-permute-done.1.prev_ref
  45.7 8.5 %shard_map.67 = (bf16[4,512,128]{2,1,0:T(8,128)(2,1)S(1)}, f32[512,128]{1,0:T(8,128)S(1)}) custom-call(s32[5]{0:T(128)S(1)} %stack.27.place_ref, bf16[512,256]{1,0:T(8,128)(2,1)S(1)} %pad_maximum_fusion.kv_ref, bf16[512,256]{1,0:T(8,128)(2,1)S(1)} %collective-permute-done.1.prev_ref, bf16[512,256]{1,0:T(8,128)(2,1)S(1)} %collective-permute-done.2.next_ref, ...), custom_call_target="tpu_custom_call" | custom-call | flops 25769803776 | bytes 4194304 | tf_op jit(solution)/shard_map/pallas_call | solution.py:229
  54.2 2.7 %all-to-all-done.1.got_ref = bf16[16,2,80,128]{3,2,1,0:T(8,128)(2,1)S(1)} async-done(((bf16[16,2,80,128]{3,2,1,0:T(8,128)(2,1)}), bf16[16,2,80,128]{3,2,1,0:T(8,128)(2,1)S(1)}, u32[]{:S(2)}, u32[]{:S(2)}) %all-to-all-start.1) | async-done | bytes 655392 | tf_op jit(solution)/shard_map/all_to_all | solution.py:386
  57.0 6.9 %shard_map.68 = (bf16[256,512]{1,0:T(8,128)(2,1)S(1)}, bf16[256,512]{1,0:T(8,128)(2,1)S(1)}) custom-call(s32[5]{0:T(128)S(1)} %stack.27.place_ref, bf16[16,2,80,128]{3,2,1,0:T(8,128)(2,1)S(1)} %all-to-all-done.1.got_ref, bf16[4,512,128]{2,1,0:T(8,128)(2,1)S(1)} %get-tuple-element.21.o_s, f32[512,128]{1,0:T(8,128)S(1)} %get-tuple-element.22.ml_s, ...), custom_call_target="tpu_custom_call" | custom-call | flops 2684354560 | bytes 4194304 | tf_op jit(solution)/shard_map/pallas_call | solution.py:307
  63.9 0.0 copy-start.2
  63.9 3.1 %collective-permute-start.3 = (bf16[256,512]{1,0:T(8,128)(2,1)S(1)}, bf16[256,512]{1,0:T(8,128)(2,1)S(1)}, u32[]{:S(2)}, u32[]{:S(2)}) collective-permute-start(bf16[256,512]{1,0:T(8,128)(2,1)S(1)} %get-tuple-element.24), channel_id=1, source_target_pairs={{0,1},{1,0},{2,3},{3,2},{4,5},{5,4},{6,7},{7,6},{8,9},{9,8},{10,11... | collective-permute-start | bytes 786440 | tf_op jit(solution)/shard_map/ppermute | solution.py:389
  67.0 1.1 %collective-permute-done.3.got_ref = bf16[256,512]{1,0:T(8,128)(2,1)S(1)} collective-permute-done((bf16[256,512]{1,0:T(8,128)(2,1)S(1)}, bf16[256,512]{1,0:T(8,128)(2,1)S(1)}, u32[]{:S(2)}, u32[]{:S(2)}) %collective-permute-start.3) | collective-permute-done | bytes 262176 | tf_op jit(solution)/shard_map/ppermute | solution.py:389
  68.2 0.0 copy-done.2
  68.2 1.1 %shard_map.69 = bf16[256,1024]{1,0:T(8,128)(2,1)} custom-call(s32[1]{0:T(128)} %bitcast.core_ref, bf16[256,512]{1,0:T(8,128)(2,1)S(1)} %get-tuple-element.23.mine_ref, bf16[256,512]{1,0:T(8,128)(2,1)S(1)} %collective-permute-done.3.got_ref, f32[1,1024]{1,0:T(1,128)S(1)} %bitcast.7), custom_call_target="tpu_custom_call" | custom-call | tf_op jit(solution)/shard_map/pallas_call | solution.py:360
  (1 shorter events, 0.0 us)
Async XLA Ops:
  2.0 27.6 %copy-start = (bf16[256,1024]{1,0:T(8,128)(2,1)S(1)}, bf16[256,1024]{1,0:T(8,128)(2,1)}, u32[]{:S(2)}) copy-start(bf16[256,1024]{1,0:T(8,128)(2,1)} %q_hbm.3) | copy-start | bytes 1572868
  2.1 21.3 %collective-permute-start = (bf16[256,768]{1,0:T(8,128)(2,1)}, bf16[256,768]{1,0:T(8,128)(2,1)S(1)}, u32[]{:S(2)}, u32[]{:S(2)}) collective-permute-start(bf16[256,768]{1,0:T(8,128)(2,1)} %get-tuple-element.16), channel_id=1, source_target_pairs={{0,1},{1,0},{2,3},{3,2},{4,5},{5,4},{6,7},{7,6},{8,9},{9,8},{10,11... | collective-permute-start | bytes 1179656 | tf_op jit(solution)/shard_map/ppermute | solution.py:378
  11.0 27.1 %all-to-all-start = ((bf16[32,8,128]{2,1,0:T(8,128)(2,1)}), bf16[32,8,128]{2,1,0:T(8,128)(2,1)S(1)}, u32[]{:S(2)}, u32[]{:S(2)}) async-start(bf16[32,8,128]{2,1,0:T(8,128)(2,1)} %get-tuple-element.15), calls=%async_computation | async-start | bytes 131072 | tf_op jit(solution)/shard_map/all_to_all | solution.py:376
  24.3 13.7 %copy-start.1 = (bf16[4,16,128]{2,1,0:T(8,128)(2,1)S(1)}, bf16[4,16,128]{2,1,0:T(8,128)(2,1)}, u32[]{:S(2)}) copy-start(bf16[4,16,128]{2,1,0:T(8,128)(2,1)} %get-tuple-element.18.fine_ref) | copy-start | bytes 49156
  24.3 21.4 %collective-permute-start.2 = (bf16[512,256]{1,0:T(8,128)(2,1)S(1)}, bf16[512,256]{1,0:T(8,128)(2,1)S(1)}, u32[]{:S(2)}, u32[]{:S(2)}) collective-permute-start(bf16[512,256]{1,0:T(8,128)(2,1)S(1)} %pad_maximum_fusion.kv_ref), channel_id=1, source_target_pairs={{2,0},{3,1},{4,2},{5,3},{6,4},{7,5},{8,6},{9,7},{10,8},{11,9},{12,... | collective-permute-start | bytes 786440 | tf_op jit(solution)/shard_map/ppermute | solution.py:382
  25.6 20.1 %collective-permute-start.1 = (bf16[512,256]{1,0:T(8,128)(2,1)S(1)}, bf16[512,256]{1,0:T(8,128)(2,1)S(1)}, u32[]{:S(2)}, u32[]{:S(2)}) collective-permute-start(bf16[512,256]{1,0:T(8,128)(2,1)S(1)} %pad_maximum_fusion.kv_ref), channel_id=1, source_target_pairs={{0,2},{1,3},{2,4},{3,5},{4,6},{5,7},{6,8},{7,9},{8,10},{9,11},{10,... | collective-permute-start | bytes 786440 | tf_op jit(solution)/shard_map/ppermute | solution.py:381
  39.1 17.9 %all-to-all-start.1 = ((bf16[16,2,80,128]{3,2,1,0:T(8,128)(2,1)}), bf16[16,2,80,128]{3,2,1,0:T(8,128)(2,1)S(1)}, u32[]{:S(2)}, u32[]{:S(2)}) async-start(bf16[16,2,80,128]{3,2,1,0:T(8,128)(2,1)} %shard_map.66), calls=%async_computation.1 | async-start | bytes 1310720 | tf_op jit(solution)/shard_map/all_to_all | solution.py:386
  63.9 4.2 %copy-start.2 = (f32[1024]{0:T(1024)S(1)}, f32[1024]{0:T(1024)}, u32[]{:S(2)}) copy-start(f32[1024]{0:T(1024)} %param.11) | copy-start | bytes 12292
  63.9 4.2 %collective-permute-start.3 = (bf16[256,512]{1,0:T(8,128)(2,1)S(1)}, bf16[256,512]{1,0:T(8,128)(2,1)S(1)}, u32[]{:S(2)}, u32[]{:S(2)}) collective-permute-start(bf16[256,512]{1,0:T(8,128)(2,1)S(1)} %get-tuple-element.24), channel_id=1, source_target_pairs={{0,1},{1,0},{2,3},{3,2},{4,5},{5,4},{6,7},{7,6},{8,9},{9,8},{10,11... | collective-permute-start | bytes 786440 | tf_op jit(solution)/shard_map/ppermute | solution.py:389
